TPU v7x, 32 devices: a whole 2x2x4 slice. The times are simulated.
32 devices in a mesh: dp: 2 (over x), pipe: 4 (over z), tensor: 4 (over y, core).
Axes of the slice: x: 2, y: 2, z: 4, core: 2. Of those that a mesh axis runs over, the one named last changes fastest.
Arguments:
- upstream: bfloat16 [4, 2, 1024, 6144], P('pipe', 'dp', 'tensor')
- inputs: bfloat16 [4, 2, 1024, 6144], P('pipe', 'dp', 'tensor')
- keys: bfloat16 [4, 2, 1024, 6144], P('pipe', 'dp', None, 'tensor')
- values: bfloat16 [4, 2, 1024, 6144], P('pipe', 'dp', None, 'tensor'), may hold values from -6 to 6
- gain: float32 [4, 6144], P('pipe'), may hold values from 0.5 to 1.5
Outputs:
- grad_inputs: bfloat16 [4, 2, 1024, 6144], P('pipe', 'dp', 'tensor')
- grad_keys: bfloat16 [4, 2, 1024, 6144], P('pipe', 'dp', None, 'tensor')
- grad_values: bfloat16 [4, 2, 1024, 6144], P('pipe', 'dp', None, 'tensor')
- grad_gain: float32 [4, 6144], P('pipe', 'tensor')
All inputs are finite; a program needn't handle non-finite values.
Results may differ from a plain program's by a relative error of at most 0.02.
The roundings to bfloat16 on the way count: a program that leaves them out, or rounds other values in their place, can miss the bound.
Values may be sent and summed in bfloat16 or wider, within the bound.
No kernel may reach another device: no remote copies, remote signals or barrier semaphores. Data moves between devices by JAX's collectives and lax.ppermute only.
A program may use at most 192 MiB of HBM per device.

v0:
```python
import math

import jax
import jax.numpy as jnp
from jax import lax
from jax.sharding import PartitionSpec as P

HEAD_DIM = 128


EPSILON = 1e-05


def from_behind(x, axis, by):
    devices = lax.axis_size(axis)
    return lax.ppermute(x, axis, [(i, (i + by) % devices) for i in range(devices)])


def attention_back(queries, key_heads, value_heads, grad_out):
    length = queries.shape[1]
    block_rows = min(512, length)
    block_total = length // block_rows
    scaling = 1.0 / math.sqrt(queries.shape[3])
    key_positions = jnp.arange(length)

    def block_step(totals, position):
        acc_keys, acc_values = totals
        offset = position * block_rows
        query_block = lax.dynamic_slice_in_dim(queries, offset, block_rows, 1)
        grad_block = lax.dynamic_slice_in_dim(grad_out, offset, block_rows, 1)
        scores = (
            jnp.einsum(
                "mqhd,mkhd->mhqk", query_block, key_heads, preferred_element_type=jnp.float32
            )
            * scaling
        )
        causal = (offset + jnp.arange(block_rows))[:, None] >= key_positions[None, :]
        scores = jnp.where(causal[None, None], scores, -jnp.inf)
        row_max = jnp.max(scores, axis=-1, keepdims=True)
        log_total = row_max + jnp.log(jnp.sum(jnp.exp(scores - row_max), axis=-1, keepdims=True))
        softmax_weights = jnp.exp(scores - log_total)
        weights_narrow = softmax_weights.astype(jnp.bfloat16)
        grad_weights = jnp.einsum(
            "mqhd,mkhd->mhqk", grad_block, value_heads, preferred_element_type=jnp.float32
        )
        row_delta = jnp.sum(softmax_weights * grad_weights, axis=-1, keepdims=True)
        grad_scores = (softmax_weights * (grad_weights - row_delta) * scaling).astype(jnp.bfloat16)
        acc_values = acc_values + jnp.einsum(
            "mhqk,mqhd->mkhd", weights_narrow, grad_block, preferred_element_type=jnp.float32
        )
        acc_keys = acc_keys + jnp.einsum(
            "mhqk,mqhd->mkhd", grad_scores, query_block, preferred_element_type=jnp.float32
        )
        grad_query = jnp.einsum(
            "mhqk,mkhd->mqhd", grad_scores, key_heads, preferred_element_type=jnp.float32
        ).astype(jnp.bfloat16)
        return ((acc_keys, acc_values), grad_query)

    empty_grads = jnp.zeros(key_heads.shape, jnp.float32)
    (grad_keys, grad_values), grad_blocks = lax.scan(
        block_step, (empty_grads, empty_grads), jnp.arange(block_total)
    )
    grad_queries = jnp.moveaxis(grad_blocks, 0, 1).reshape(queries.shape)
    return (grad_queries, grad_keys, grad_values)


def body(upstream, inputs, keys, values, gain):
    tensor_size = lax.axis_size("tensor")
    tensor_rank = lax.axis_index("tensor")
    batches = inputs.shape[1]
    tokens_local = inputs.shape[2]
    columns = inputs.shape[3] // tensor_size
    length = keys.shape[2]
    inputs_wide = inputs.astype(jnp.float32)
    root_mean = jnp.sqrt(jnp.mean(inputs_wide * inputs_wide, axis=-1, keepdims=True) + EPSILON)
    normed = inputs_wide / root_mean
    normed_b = normed.astype(jnp.bfloat16)
    normed_heads = lax.all_to_all(normed_b, "tensor", split_axis=3, concat_axis=2, tiled=True)
    full_rows = lax.all_gather(upstream, "tensor", axis=2, tiled=True)
    arrived = from_behind(full_rows, "pipe", -1)
    incoming = lax.dynamic_slice_in_dim(arrived, tensor_rank * tokens_local, tokens_local, 2)
    grad_out = lax.dynamic_slice_in_dim(arrived, tensor_rank * columns, columns, 3)
    gain_columns = lax.dynamic_slice_in_dim(gain, tensor_rank * columns, columns, 1)
    queries = (normed_heads.astype(jnp.float32) * gain_columns[:, None, None, :]).astype(
        jnp.bfloat16
    )
    head_shape = (batches, length, columns // HEAD_DIM, HEAD_DIM)
    grad_queries, grad_keys, grad_values = attention_back(
        queries[0].reshape(head_shape),
        keys[0].reshape(head_shape),
        values[0].reshape(head_shape),
        grad_out[0].reshape(head_shape),
    )
    grad_flat = grad_queries.reshape(1, batches, length, columns)
    partial_gain = jnp.sum(
        grad_flat.astype(jnp.float32) * normed_heads.astype(jnp.float32), axis=(1, 2)
    )
    grad_gain = lax.psum(partial_gain, "dp")
    grad_rows = lax.all_to_all(grad_flat, "tensor", split_axis=2, concat_axis=3, tiled=True)
    scaled = grad_rows.astype(jnp.float32) * gain[:, None, None, :]
    grad_inputs = (
        incoming.astype(jnp.float32)
        + (scaled - normed * jnp.mean(scaled * normed, axis=-1, keepdims=True)) / root_mean
    )
    return (
        grad_inputs.astype(jnp.bfloat16),
        grad_keys.reshape(keys.shape).astype(jnp.bfloat16),
        grad_values.reshape(values.shape).astype(jnp.bfloat16),
        grad_gain,
    )


def solution(mesh):
    in_specs = (
        P("pipe", "dp", "tensor", None),
        P("pipe", "dp", "tensor", None),
        P("pipe", "dp", None, "tensor"),
        P("pipe", "dp", None, "tensor"),
        P("pipe", None),
    )
    out_specs = (
        P("pipe", "dp", "tensor", None),
        P("pipe", "dp", None, "tensor"),
        P("pipe", "dp", None, "tensor"),
        P("pipe", "tensor"),
    )
    return jax.shard_map(body, mesh=mesh, in_specs=in_specs, out_specs=out_specs, check_vma=False)
```

profile of v0, /device:TPU:0, one launch (start us, length us, event | category | flops | bytes accessed | tf_op | source)
XLA Modules:
  0.0 841.0 jit_solution(10010612940207399717)
XLA Ops:
  11.9 86.6 %all-gather.2.cloned.1.call-done = bf16[1,1,1024,6144]{2,3,1,0:T(8,128)(2,1)} async-done(((bf16[1,1,256,6144]{2,3,1,0:T(8,128)(2,1)}), bf16[1,1,1024,6144]{2,3,1,0:T(8,128)(2,1)}) %all-gather.2.cloned.1.call-update) | async-done | bytes 12582928 | tf_op jit(solution)/shard_map/all_gather | solution.py:79
  106.5 37.2 %copy.63 = bf16[1,1,256,6144]{2,1,0,3:T(2,128)(2,1)} copy(bf16[1,1,256,6144]{2,3,1,0:T(8,128)(2,1)S(1)} %fusion.58) | data formatting | bytes 6291456 | tf_op jit(solution)/shard_map/convert_element_type | solution.py:77
  144.3 31.5 %reduce.11 = bf16[6144,256]{1,0:T(8,128)(2,1)S(1)} reduce(bf16[6144,1,1,256]{3,2,1,0:T(2,128)(2,1)} %bitcast.111, bf16[]{:T(256)} %broadcast.162), dimensions={1,2}, to_apply=%bitcast.85.reduce_sub_computation | reduce | bytes 6291458
  178.3 5.0 all-to-all-start
  198.3 22.0 %all-to-all-done = bf16[4,2,196608]{2,1,0:T(2,128)(2,1)} async-done(((bf16[4,2,196608]{2,1,0:T(2,128)(2,1)}), bf16[4,2,196608]{2,1,0:T(2,128)(2,1)}, u32[]{:S(2)}, u32[]{:S(2)}) %all-to-all-start) | async-done | bytes 3145760 | tf_op jit(solution)/shard_map/all_to_all | solution.py:78
  220.3 6.2 reshape.278
  226.5 9.6 %copy.61 = f32[1,1,256,4,1536]{2,3,4,1,0:T(4,128)} copy(bf16[1,1,256,4,1536]{2,1,4,3,0:T(2,128)(2,1)} %bitcast.113) | data formatting | bytes 9437184 | tf_op jit(solution)/shard_map/convert_element_type | solution.py:84
  236.1 8.3 reshape.265
  249.2 122.9 %collective-permute-done = bf16[1,1,1024,6144]{2,3,1,0:T(8,128)(2,1)} collective-permute-done((bf16[1,1,1024,6144]{2,3,1,0:T(8,128)(2,1)}, bf16[1,1,1024,6144]{2,3,1,0:T(8,128)(2,1)}, u32[]{:S(2)}, u32[]{:S(2)}) %collective-permute-start) | collective-permute-done | bytes 12582944 | tf_op jit(solution)/shard_map/ppermute | solution.py:16
  376.0 325.2 %while.15 = (s32[]{:T(128)}, f32[1,1024,12,128]{1,3,2,0:T(8,128)}, f32[1,1024,12,128]{1,3,2,0:T(8,128)}, bf16[2,1,512,12,128]{4,2,3,1,0:T(8,128)(2,1)}, s32[2]{0...) while((s32[]{:T(128)}, f32[1,1024,12,128]{1,3,2,0:T(8,128)}, ...), condition=%wide.region_5.6_spmd.clone, body=%wide.region_1.5_spmd.clone.sunk | while | flops 8268292608 | bytes 376221984 | solution.py:60
  390.4 11.8 %fusion.77 = f32[12,512,1024]{2,1,0:T(8,128)} fusion(bf16[1,1024,12,128]{3,1,2,0:T(8,128)(2,1)S(1)} %get-tuple-element.232, bf16[1,1024,12,128]{1,3,2,0:T(8,128)(2,1)} %get-tuple-element.231, s32[]{:T(128)S(6)} %select_n.75), kind=kOutput, calls=%fused_computation.15.clone.1 | convolution fusion | flops 1610612736 | bytes 29884420 | tf_op jit(solution)/shard_map/while/body/eval_jaxpr/mqhd,mkhd->mhqk/dot_general | solution.py:43
  402.2 10.8 %fusion.78 = (f32[12,512]{1,0:T(8,128)S(1)}, f32[12,512,1024]{2,1,0:T(8,128)}) fusion(pred[512,1024]{1,0:T(8,128)(4,1)S(1)} %iota_compare_fusion.2, bf16[1,1024,12,128]{3,1,2,0:T(8,128)(2,1)S(1)} %copy-done.1, bf16[1,1024,12,128]{1,3,2,0:T(8,128)(2,1)S(1)} %copy-done.5, s32[]{:T(128)S(6)} %select_n.75), kind=kOutput, calls=%fused_computation.8.clone.1 | convolution fusion | flops 1629480960 | bytes 30433284 | tf_op jit(solution)/shard_map/while/body/eval_jaxpr/mqhd,mkhd->mhqk/dot_general | solution.py:32
  413.0 11.8 %exponential_reduce_fusion.2 = f32[12,512]{1,0:T(8,128)S(1)} fusion(f32[12,512,1024]{2,1,0:T(8,128)} %get-tuple-element.197, f32[12,512]{1,0:T(8,128)S(1)} %get-tuple-element.196, pred[512,1024]{1,0:T(8,128)(4,1)S(1)} %iota_compare_fusion.2), kind=kLoop, calls=%fused_computation.6.clone.1 | loop fusion | flops 25159680 | bytes 25739264 | tf_op jit(solution)/shard_map/while/body/eval_jaxpr/reduce_sum | solution.py:40
  424.9 54.0 %bitcast_dynamic-update-slice_fusion.2 = bf16[2,1,512,12,128]{4,2,3,1,0:T(8,128)(2,1)} fusion(bf16[2,1,512,12,128]{4,2,3,1,0:T(8,128)(2,1)} %get-tuple-element.214, s32[]{:T(128)S(6)} %copy.69, bf16[1,1024,12,128]{3,1,2,0:T(8,128)(2,1)} %get-tuple-element.230, f32[12,512,1024]{2,1,0:T(8,128)} %fusion.77, f32[12,512]{1,0:T(8,128)S(1)} %log_add_fusion.2, ...), kind=kOutput, calls=%fused_computation.26.clone.1 | convolution fusion | flops 1680612352 | bytes 106496000 | tf_op jit(solution)/shard_map/while/body/eval_jaxpr/mhqk,mkhd->mqhd/dot_general | solution.py:54
  478.9 50.6 %bitcast_add_fusion.4 = f32[1,1024,12,128]{1,3,2,0:T(8,128)} fusion(f32[1,1024,12,128]{1,3,2,0:T(8,128)} %get-tuple-element.212, pred[]{:T(512)S(6)} %compare.3, f32[12,512,1024]{2,1,0:T(8,128)} %fusion.77, f32[12,512]{1,0:T(8,128)S(1)} %log_add_fusion.2, f32[12,512,1024]{2,1,0:T(8,128)} %get-tuple-element.197, pred[512,1024]{1,0:T(8,128)(4,1)} %copy-done, ...), kind=kOutput, calls=%fused_computation.14.clone.1 | convolution fusion | flops 1682971648 | bytes 115933192 | tf_op jit(solution)/shard_map/while/body/eval_jaxpr/mhqk,mqhd->mkhd/dot_general | solution.py:51
  529.5 14.3 %bitcast_add_fusion.5 = f32[1,1024,12,128]{1,3,2,0:T(8,128)} fusion(f32[1,1024,12,128]{1,3,2,0:T(8,128)} %get-tuple-element.213, pred[]{:T(512)S(6)} %compare.3, f32[12,512]{1,0:T(8,128)S(1)} %log_add_fusion.2, f32[12,512,1024]{2,1,0:T(8,128)} %get-tuple-element.197, pred[512,1024]{1,0:T(8,128)(4,1)} %copy-done, ...), kind=kOutput, calls=%fused_computation.13.clone.1 | convolution fusion | flops 1638924288 | bytes 39870468 | tf_op jit(solution)/shard_map/while/body/eval_jaxpr/mhqk,mqhd->mkhd/dot_general | solution.py:48
  545.4 11.8 %fusion.77 = f32[12,512,1024]{2,1,0:T(8,128)} fusion(bf16[1,1024,12,128]{3,1,2,0:T(8,128)(2,1)S(1)} %get-tuple-element.232, bf16[1,1024,12,128]{1,3,2,0:T(8,128)(2,1)} %get-tuple-element.231, s32[]{:T(128)S(6)} %select_n.75), kind=kOutput, calls=%fused_computation.15.clone.1 | convolution fusion | flops 1610612736 | bytes 29884420 | tf_op jit(solution)/shard_map/while/body/eval_jaxpr/mqhd,mkhd->mhqk/dot_general | solution.py:43
  557.2 10.8 %fusion.78 = (f32[12,512]{1,0:T(8,128)S(1)}, f32[12,512,1024]{2,1,0:T(8,128)}) fusion(pred[512,1024]{1,0:T(8,128)(4,1)S(1)} %iota_compare_fusion.2, bf16[1,1024,12,128]{3,1,2,0:T(8,128)(2,1)S(1)} %copy-done.1, bf16[1,1024,12,128]{1,3,2,0:T(8,128)(2,1)S(1)} %copy-done.5, s32[]{:T(128)S(6)} %select_n.75), kind=kOutput, calls=%fused_computation.8.clone.1 | convolution fusion | flops 1629480960 | bytes 30433284 | tf_op jit(solution)/shard_map/while/body/eval_jaxpr/mqhd,mkhd->mhqk/dot_general | solution.py:32
  568.0 11.8 %exponential_reduce_fusion.2 = f32[12,512]{1,0:T(8,128)S(1)} fusion(f32[12,512,1024]{2,1,0:T(8,128)} %get-tuple-element.197, f32[12,512]{1,0:T(8,128)S(1)} %get-tuple-element.196, pred[512,1024]{1,0:T(8,128)(4,1)S(1)} %iota_compare_fusion.2), kind=kLoop, calls=%fused_computation.6.clone.1 | loop fusion | flops 25159680 | bytes 25739264 | tf_op jit(solution)/shard_map/while/body/eval_jaxpr/reduce_sum | solution.py:40
  579.9 54.0 %bitcast_dynamic-update-slice_fusion.2 = bf16[2,1,512,12,128]{4,2,3,1,0:T(8,128)(2,1)} fusion(bf16[2,1,512,12,128]{4,2,3,1,0:T(8,128)(2,1)} %get-tuple-element.214, s32[]{:T(128)S(6)} %copy.69, bf16[1,1024,12,128]{3,1,2,0:T(8,128)(2,1)} %get-tuple-element.230, f32[12,512,1024]{2,1,0:T(8,128)} %fusion.77, f32[12,512]{1,0:T(8,128)S(1)} %log_add_fusion.2, ...), kind=kOutput, calls=%fused_computation.26.clone.1 | convolution fusion | flops 1680612352 | bytes 106496000 | tf_op jit(solution)/shard_map/while/body/eval_jaxpr/mhqk,mkhd->mqhd/dot_general | solution.py:54
  633.9 50.6 %bitcast_add_fusion.4 = f32[1,1024,12,128]{1,3,2,0:T(8,128)} fusion(f32[1,1024,12,128]{1,3,2,0:T(8,128)} %get-tuple-element.212, pred[]{:T(512)S(6)} %compare.3, f32[12,512,1024]{2,1,0:T(8,128)} %fusion.77, f32[12,512]{1,0:T(8,128)S(1)} %log_add_fusion.2, f32[12,512,1024]{2,1,0:T(8,128)} %get-tuple-element.197, pred[512,1024]{1,0:T(8,128)(4,1)} %copy-done, ...), kind=kOutput, calls=%fused_computation.14.clone.1 | convolution fusion | flops 1682971648 | bytes 115933192 | tf_op jit(solution)/shard_map/while/body/eval_jaxpr/mhqk,mqhd->mkhd/dot_general | solution.py:51
  684.5 16.4 %bitcast_add_fusion.5 = f32[1,1024,12,128]{1,3,2,0:T(8,128)} fusion(f32[1,1024,12,128]{1,3,2,0:T(8,128)} %get-tuple-element.213, pred[]{:T(512)S(6)} %compare.3, f32[12,512]{1,0:T(8,128)S(1)} %log_add_fusion.2, f32[12,512,1024]{2,1,0:T(8,128)} %get-tuple-element.197, pred[512,1024]{1,0:T(8,128)(4,1)} %copy-done, ...), kind=kOutput, calls=%fused_computation.13.clone.1 | convolution fusion | flops 1638924288 | bytes 39870468 | tf_op jit(solution)/shard_map/while/body/eval_jaxpr/mhqk,mqhd->mkhd/dot_general | solution.py:48
  701.2 6.1 copy.53
  707.3 19.0 %reshape.275 = bf16[1,1,1024,1536]{3,1,0,2:T(2,128)(2,1)} reshape(bf16[2,1,512,12,128]{4,3,2,0,1:T(8,128)(2,1)} %copy.53) | data formatting | bytes 6291456 | tf_op jit(solution)/shard_map/reshape;reshape;transpose | solution.py:94
  726.3 20.3 %reduce.12 = bf16[1024,1536]{1,0:T(8,128)(2,1)S(1)} reduce(bf16[1024,1,1,1536]{3,2,1,0:T(2,128)(2,1)} %bitcast.112, bf16[]{:T(256)} %broadcast.162), dimensions={1,2}, to_apply=%bitcast.76.reduce_sub_computation | reduce | bytes 6291458
  754.8 9.5 %reshape.267 = f32[2,1,512,12,128]{2,0,4,3,1:T(2,128)} reshape(f32[1,1,4,256,1536]{3,2,4,1,0:T(4,128)} %bitcast.109) | data formatting | bytes 12582912 | tf_op jit(solution)/shard_map/convert_element_type | solution.py:84
  764.3 5.6 copy.43
  776.1 5.1 convert_element_type.150
  785.8 8.6 %multiply_reduce_fusion.1 = f32[12,128]{1,0:T(8,128)S(1)} fusion(f32[2,1,512,12,128]{2,0,4,3,1:T(2,128)} %reshape.267, bf16[2,1,512,12,128]{2,0,4,3,1:T(2,128)(2,1)S(1)} %copy-done.7), kind=kLoop, calls=%fused_computation.51 | loop fusion | flops 4717056 | bytes 9443328 | tf_op jit(solution)/shard_map/reduce_sum | solution.py:95
  794.4 5.7 psum.7
  800.2 6.2 reshape.280
  813.5 6.8 copy.46
  (70 shorter events, 81.1 us)
Async XLA Ops:
  7.2 91.3 %all-gather.2.cloned.1.call-start = ((), (), s32[]{:S(2)}) async-start(), calls=%async_computation.2 | async-start | bytes 15728640 | tf_op jit(solution)/shard_map/all_gather | solution.py:79
  98.5 273.7 %collective-permute-start = (bf16[1,1,1024,6144]{2,3,1,0:T(8,128)(2,1)}, bf16[1,1,1024,6144]{2,3,1,0:T(8,128)(2,1)}, u32[]{:S(2)}, u32[]{:S(2)}) collective-permute-start(bf16[1,1,1024,6144]{2,3,1,0:T(8,128)(2,1)} %all-gather.2.cloned.1.call-done), channel_id=1, source_target_pairs={{0,12},{4,0},{8,4},{12,8},{1,13},{5,1},{9,5},{13,9},{2,14},{6,2},{... | collective-permute-start | bytes 37748744 | tf_op jit(solution)/shard_map/ppermute | solution.py:16
  105.0 38.7 %copy-start.2 = (bf16[1,1,256,6144]{2,3,1,0:T(8,128)(2,1)}, bf16[1,1,256,6144]{2,3,1,0:T(8,128)(2,1)S(1)}, u32[]{:S(2)}) copy-start(bf16[1,1,256,6144]{2,3,1,0:T(8,128)(2,1)S(1)} %copy.34) | copy-start | bytes 9437188
  105.9 37.9 %copy-start.9 = (f32[256]{0:T(256)}, f32[256]{0:T(256)S(1)}, u32[]{:S(2)}) copy-start(f32[256]{0:T(256)S(1)} %add_sqrt_fusion) | copy-start | bytes 3076
  178.3 42.0 %all-to-all-start = ((bf16[4,2,196608]{2,1,0:T(2,128)(2,1)}), bf16[4,2,196608]{2,1,0:T(2,128)(2,1)}, u32[]{:S(2)}, u32[]{:S(2)}) async-start(bf16[4,2,196608]{2,1,0:T(2,128)(2,1)} %reshape.277), calls=%async_computation | async-start | bytes 6291456 | tf_op jit(solution)/shard_map/all_to_all | solution.py:78
  390.4 22.6 %copy-start = (pred[512,1024]{1,0:T(8,128)(4,1)}, pred[512,1024]{1,0:T(8,128)(4,1)S(1)}, u32[]{:S(2)}) copy-start(pred[512,1024]{1,0:T(8,128)(4,1)S(1)} %iota_compare_fusion.2) | copy-start | bytes 1572868 | tf_op jit(solution)/shard_map/while
  390.4 11.8 %copy-start.1 = (bf16[1,1024,12,128]{3,1,2,0:T(8,128)(2,1)S(1)}, bf16[1,1024,12,128]{3,1,2,0:T(8,128)(2,1)}, u32[]{:S(2)}) copy-start(bf16[1,1024,12,128]{3,1,2,0:T(8,128)(2,1)} %get-tuple-element.230) | copy-start | bytes 9437188 | tf_op jit(solution)/shard_map/while
  390.4 11.8 %copy-start.5 = (bf16[1,1024,12,128]{1,3,2,0:T(8,128)(2,1)S(1)}, bf16[1,1024,12,128]{1,3,2,0:T(8,128)(2,1)}, u32[]{:S(2)}) copy-start(bf16[1,1024,12,128]{1,3,2,0:T(8,128)(2,1)} %get-tuple-element.229) | copy-start | bytes 9437188 | tf_op jit(solution)/shard_map/while
  545.4 22.6 %copy-start = (pred[512,1024]{1,0:T(8,128)(4,1)}, pred[512,1024]{1,0:T(8,128)(4,1)S(1)}, u32[]{:S(2)}) copy-start(pred[512,1024]{1,0:T(8,128)(4,1)S(1)} %iota_compare_fusion.2) | copy-start | bytes 1572868 | tf_op jit(solution)/shard_map/while
  545.4 11.8 %copy-start.1 = (bf16[1,1024,12,128]{3,1,2,0:T(8,128)(2,1)S(1)}, bf16[1,1024,12,128]{3,1,2,0:T(8,128)(2,1)}, u32[]{:S(2)}) copy-start(bf16[1,1024,12,128]{3,1,2,0:T(8,128)(2,1)} %get-tuple-element.230) | copy-start | bytes 9437188 | tf_op jit(solution)/shard_map/while
  545.4 11.8 %copy-start.5 = (bf16[1,1024,12,128]{1,3,2,0:T(8,128)(2,1)S(1)}, bf16[1,1024,12,128]{1,3,2,0:T(8,128)(2,1)}, u32[]{:S(2)}) copy-start(bf16[1,1024,12,128]{1,3,2,0:T(8,128)(2,1)} %get-tuple-element.229) | copy-start | bytes 9437188 | tf_op jit(solution)/shard_map/while
  750.1 50.0 %all-to-all-start.1 = ((bf16[4,2,196608]{2,1,0:T(2,128)(2,1)}), bf16[4,2,196608]{2,1,0:T(2,128)(2,1)}, u32[]{:S(2)}, u32[]{:S(2)}) async-start(bf16[4,2,196608]{2,1,0:T(2,128)(2,1)} %reshape.279), calls=%async_computation.1 | async-start | bytes 6291456 | tf_op jit(solution)/shard_map/all_to_all | solution.py:99
  754.8 9.5 %copy-start.6 = (bf16[2,1,512,12,128]{4,2,3,1,0:T(8,128)(2,1)S(1)}, bf16[2,1,512,12,128]{4,2,3,1,0:T(8,128)(2,1)}, u32[]{:S(2)}) copy-start(bf16[2,1,512,12,128]{4,2,3,1,0:T(8,128)(2,1)} %get-tuple-element.58) | copy-start | bytes 9437188
  776.1 9.7 %copy-start.7 = (bf16[2,1,512,12,128]{2,0,4,3,1:T(2,128)(2,1)S(1)}, bf16[2,1,512,12,128]{2,0,4,3,1:T(2,128)(2,1)}, u32[]{:S(2)}) copy-start(bf16[2,1,512,12,128]{2,0,4,3,1:T(2,128)(2,1)} %copy.43) | copy-start | bytes 9437188
  813.5 6.8 copy-start.3
  813.5 6.8 copy-start.8
  813.5 6.8 copy-start.10
  820.2 4.6 copy-start.4
Sparse Core Ops, SparseCore 0:
  12.0 86.4 all-gather.1
where the time goes:
time: 843 us; the launch traced here: 841 us
  matrix products  285 us (34%)
  waiting for transfers between devices  232 us (28%)
  local copies, waits for them, and re-layouts  166 us (20%)
  other arithmetic  111 us (13%)
  loops' own time  14.5 us (2%)
  between operations  14.4 us (2%)
  starting transfers between devices  13.1 us (2%)
    ppermute x1, waiting for transfers between devices, from_behind(): lax.ppermute(x, axis, [(i, (i + by) % devices) for i in range(devices)])  123 us
    dot_general x2, matrix products, block_step(): jnp.einsum('mhqk,mkhd->mqhd', grad_scores, key_heads, preferred_element_t...  108 us
    dot_general x2, matrix products, block_step(): jnp.einsum('mhqk,mqhd->mkhd', grad_scores, query_block, preferred_element...  101 us
    all_gather x1, waiting for transfers between devices, body(): full_rows = lax.all_gather(upstream, 'tensor', axis=2, tiled=True)  86.6 us
    unnamed x31, local copies, waits for them, and re-layouts  54.1 us
    unnamed x4, other arithmetic  51.8 us
    convert_element_type x1, local copies, waits for them, and re-layouts, body(): normed_b = normed.astype(jnp.bfloat16)  37.2 us
    dot_general x2, matrix products, block_step(): jnp.einsum('mhqk,mqhd->mkhd', weights_narrow, grad_block, preferred_eleme...  30.7 us
  transfers between devices with their start and end apart: 4, of which 3 were waited for; matrix products, arithmetic and copies ran while one was open for 19% of the time, Pallas kernels for 0%

commit v1 on v0

v1 whole, which is shorter than its diff:
```python
import functools
import math

import jax
import jax.numpy as jnp
from jax import lax
from jax.experimental import pallas as pl
from jax.experimental.pallas import tpu as pltpu
from jax.sharding import PartitionSpec as P

HEAD_DIM = 128
EPSILON = 1e-05
CHUNKS = 3
BLOCK = 256
HEADS_A_STEP = 2
MIB = 1 << 20


def params(limit):
    return pltpu.CompilerParams(vmem_limit_bytes=limit * MIB)


def cost(flops, moved, exps=0):
    return pl.CostEstimate(flops=flops, bytes_accessed=moved, transcendentals=exps)


def made(shape, dtype=jnp.bfloat16):
    return jax.ShapeDtypeStruct(shape, dtype)


def cut(columns, chunks):
    heads = columns // HEAD_DIM
    chunks = min(chunks, heads)
    bounds = [-(-heads * c // chunks) * HEAD_DIM for c in range(chunks + 1)]
    return [(start, end - start) for start, end in zip(bounds, bounds[1:])]


def pinned(x):
    return pltpu.with_memory_space_constraint(x, pltpu.HBM)


def prepare_kernel(shares, ranks, steps, rank_ref, upstream_ref, inputs_ref, *refs):
    *out_refs, upstream_held, inputs_held, arrived = refs
    handed_refs, normed_refs = out_refs[: len(shares)], out_refs[len(shares) :]
    block_rows = inputs_ref.shape[0] // steps
    columns = inputs_ref.shape[1] // ranks
    step = pl.program_id(0)

    def copies(i):
        down = pl.ds(pl.multiple_of(i * block_rows, block_rows), block_rows)
        return [
            pltpu.make_async_copy(source.at[down, :], held.at[down, :], arrived.at[n, i])
            for n, (source, held) in enumerate(((inputs_ref, inputs_held), (upstream_ref, upstream_held)))
        ]

    @pl.when(step == 0)
    def _():
        for i in range(steps):
            for copy in copies(i):
                copy.start()

    for copy in copies(step):
        copy.wait()
    down = pl.ds(pl.multiple_of(step * block_rows, block_rows), block_rows)
    x = inputs_held[down, :].astype(jnp.float32)
    inverse = 1.0 / jnp.sqrt(jnp.mean(x * x, axis=-1, keepdims=True) + EPSILON)
    for c, (start, wide) in enumerate(shares):
        for k in range(ranks):
            at = pl.ds(pl.multiple_of((rank_ref[0] ^ k) * columns + start, HEAD_DIM), wide)
            handed_refs[c][k] = upstream_held[down, at]
            piece = inputs_held[down, at].astype(jnp.float32)
            normed_refs[c * ranks + k][...] = (piece * inverse).astype(jnp.bfloat16)


def prepare(rank, upstream, inputs, shares, ranks, block_rows):
    length, features = inputs.shape
    steps = length // block_rows
    whole = pl.BlockSpec(memory_space=pl.ANY)
    outs = pl.pallas_call(
        functools.partial(prepare_kernel, shares, ranks, steps),
        grid_spec=pltpu.PrefetchScalarGridSpec(
            num_scalar_prefetch=1,
            grid=(steps,),
            in_specs=[whole, whole],
            out_specs=[pl.BlockSpec((ranks, block_rows, wide), lambda i, _: (0, i, 0)) for _, wide in shares]
            + [pl.BlockSpec((block_rows, wide), lambda i, _: (i, 0)) for _, wide in shares for _ in range(ranks)],
            scratch_shapes=[pltpu.VMEM((length, features), jnp.bfloat16)] * 2
            + [pltpu.SemaphoreType.DMA((2, steps))],
        ),
        out_shape=[made((ranks, length, wide)) for _, wide in shares]
        + [
            made((length, wide)) if k else pltpu.HBM((length, wide), jnp.bfloat16)
            for _, wide in shares
            for k in range(ranks)
        ],
        compiler_params=params(14),
        cost_estimate=cost(4 * inputs.size, 8 * inputs.size),
    )(rank, pinned(upstream), pinned(inputs))
    normed = outs[len(shares) :]
    return outs[: len(shares)], [normed[c * ranks : (c + 1) * ranks] for c in range(len(shares))]


def folded(x):
    return jnp.sum(x.reshape(x.shape[0] // 8, 8, x.shape[1]), axis=0)


def attention_kernel(ranks, rank_ref, *refs):
    normed_refs, grad_out_refs = refs[:ranks], refs[ranks : 2 * ranks]
    keys_ref, values_ref, gain_ref = refs[2 * ranks : 2 * ranks + 3]
    *grad_queries_refs, grad_keys_ref, grad_values_ref, grad_gain_ref, normed_ref, out_ref, turned_ref = refs[
        -ranks - 6 :
    ]
    tokens = grad_queries_refs[0].shape[0]
    length, wide = keys_ref.shape
    block = min(BLOCK, length)
    blocks = length // block
    scaling = 1.0 / math.sqrt(HEAD_DIM)
    base = scaling * math.log2(math.e)

    def rows_of(k):
        return pl.ds(pl.multiple_of((rank_ref[0] ^ k) * tokens, tokens), tokens)

    for k in range(ranks):
        normed_ref[rows_of(k), :] = normed_refs[k][...]
        out_ref[rows_of(k), :] = grad_out_refs[k][0] if k == 0 else grad_out_refs[k][...]

    key_at = lax.broadcasted_iota(jnp.int32, (block, block), 0)
    query_at = lax.broadcasted_iota(jnp.int32, (block, block), 1)
    allowed = key_at <= query_at
    across = (((1,), (1,)), ((), ()))

    def rows(x, i):
        return x[i * block : (i + 1) * block]

    heads = []
    for start in range(0, wide, HEAD_DIM):
        at = slice(start, start + HEAD_DIM)
        keys = keys_ref[:, at]
        heads.append(
            dict(
                at=at,
                queries=(normed_ref[:, at].astype(jnp.float32) * gain_ref[:, at]).astype(jnp.bfloat16),
                grad_out=out_ref[:, at],
                keys=keys,
                values=values_ref[:, at],
                keys_turned=keys.T,
                grad_keys=[None] * blocks,
                grad_values=[None] * blocks,
            )
        )

    def product(head, i, j):
        score = lax.dot_general(
            rows(head["keys"], j), rows(head["queries"], i), across, preferred_element_type=jnp.float32
        )
        weighed = lax.dot_general(
            rows(head["values"], j), rows(head["grad_out"], i), across, preferred_element_type=jnp.float32
        )
        score = jnp.where(allowed, score, -jnp.inf) if j == i else score
        return score, weighed, jnp.max(score.reshape(block // 8, 8, block), axis=0)

    def joined(x, y):
        return y if x is None else x + y

    stages = [(head, i) for head in heads for i in range(blocks)]
    ready = [product(*stages[0], j) for j in range(stages[0][1] + 1)]
    for at, (head, i) in enumerate(stages):
        tiles, ready = ready, []
        later = [(*stages[at + 1], j) for j in range(stages[at + 1][1] + 1)] if at + 1 < len(stages) else []
        top = functools.reduce(jnp.maximum, [t[2] for t in tiles])
        shift = jnp.max(top, axis=0, keepdims=True) * base
        exps, total, slope = [], None, None
        for j, (score, weighed, _) in enumerate(tiles):
            e = jnp.exp2(score * base - shift)
            exps.append(e)
            total = joined(total, folded(e))
            slope = joined(slope, folded(e * weighed))
            if later:
                ready.append(product(*later.pop(0)))
        ready += [product(*one) for one in later]
        inverse = 1.0 / jnp.sum(total, axis=0, keepdims=True)
        delta = jnp.sum(slope, axis=0, keepdims=True) * inverse
        query, grad = rows(head["queries"], i), rows(head["grad_out"], i)
        turned = None
        for j, (_, weighed, _) in enumerate(tiles):
            weights = exps[j] * inverse
            narrow = weights.astype(jnp.bfloat16)
            slopes = (weights * (weighed - delta) * scaling).astype(jnp.bfloat16)
            head["grad_values"][j] = joined(
                head["grad_values"][j], jnp.dot(narrow, grad, preferred_element_type=jnp.float32)
            )
            head["grad_keys"][j] = joined(
                head["grad_keys"][j], jnp.dot(slopes, query, preferred_element_type=jnp.float32)
            )
            keys_turned = head["keys_turned"][:, j * block : (j + 1) * block]
            turned = joined(turned, jnp.dot(keys_turned, slopes, preferred_element_type=jnp.float32))
        turned_ref[i * block : (i + 1) * block, head["at"]] = turned.T.astype(jnp.bfloat16)
        if i == blocks - 1:
            for j in range(blocks):
                down = slice(j * block, (j + 1) * block)
                grad_keys_ref[down, head["at"]] = head["grad_keys"][j].astype(jnp.bfloat16)
                grad_values_ref[down, head["at"]] = head["grad_values"][j].astype(jnp.bfloat16)

    grad_gain_ref[...] = jnp.sum(
        folded(turned_ref[...].astype(jnp.float32) * normed_ref[...].astype(jnp.float32)), axis=0, keepdims=True
    )
    for k, grad_queries_ref in enumerate(grad_queries_refs):
        grad_queries_ref[...] = turned_ref[rows_of(k), :]


def attention_back(share, rank, normed, grad_out, keys, values, gain, earlier):
    start, wide = share
    heads = wide // HEAD_DIM
    step = math.gcd(math.gcd(start, wide), HEADS_A_STEP * HEAD_DIM)
    first = start // step
    ranks, tokens = len(normed), normed[0].shape[0]
    length = keys.shape[0]
    own = pl.BlockSpec((tokens, step), lambda h, _: (0, h))
    first_piece = pl.BlockSpec((1, tokens, step), lambda h, _: (0, 0, h))
    placed = pl.BlockSpec((length, step), lambda h, _: (0, first + h))
    pairs = length * length * heads
    outs = pl.pallas_call(
        functools.partial(attention_kernel, ranks),
        grid_spec=pltpu.PrefetchScalarGridSpec(
            num_scalar_prefetch=1,
            grid=(wide // step,),
            in_specs=[own] * ranks
            + [first_piece]
            + [own] * (ranks - 1)
            + [placed, placed, pl.BlockSpec((1, step), lambda h, _: (0, first + h))]
            + [pl.BlockSpec(memory_space=pl.ANY)] * len(earlier),
            out_specs=[own] * ranks
            + [placed, placed, pl.BlockSpec((1, step), lambda h, _: (0, h))],
            scratch_shapes=[pltpu.VMEM((length, step), jnp.bfloat16)] * 3,
        ),
        out_shape=[made((tokens, wide))] * ranks
        + [pltpu.HBM(keys.shape, jnp.bfloat16)] * 2
        + [made((1, wide), jnp.float32)],
        input_output_aliases={2 * ranks + 4 + i: ranks + i for i in range(len(earlier))},
        compiler_params=params(20),
        cost_estimate=cost(10 * pairs * HEAD_DIM, 8 * pairs, pairs),
    )(rank, *normed, *grad_out, pinned(keys), pinned(values), gain, *earlier)
    return outs[:ranks], outs[ranks : ranks + 2], outs[-1]


def finish_kernel(shares, ranks, rank_ref, inputs_ref, gain_ref, *refs):
    incoming_refs, grad_refs, out_ref = refs[: len(shares)], refs[len(shares) : -1], refs[-1]
    features = inputs_ref.shape[1]
    columns = features // ranks

    def pieces():
        for c, (start, wide) in enumerate(shares):
            for k in range(ranks):
                at = pl.ds(pl.multiple_of((rank_ref[0] ^ k) * columns + start, HEAD_DIM), wide)
                x = inputs_ref[:, at].astype(jnp.float32)
                scaled = grad_refs[c * ranks + k][...].astype(jnp.float32) * gain_ref[:, at]
                yield c, k, at, x, scaled

    def along(terms):
        return jnp.sum(sum(terms), axis=-1, keepdims=True)

    def lanes(x):
        return sum(x[:, i : i + HEAD_DIM] for i in range(0, x.shape[1], HEAD_DIM))

    squares, products = [], []
    for _, _, _, x, scaled in pieces():
        squares.append(lanes(x * x))
        products.append(lanes(scaled * x))
    inverse = 1.0 / jnp.sqrt(along(squares) / features + EPSILON)
    slope = along(products) / features * inverse * inverse * inverse
    for c, k, at, x, scaled in pieces():
        incoming = incoming_refs[c][k].astype(jnp.float32)
        out_ref[:, at] = (incoming + (scaled * inverse - x * slope)).astype(jnp.bfloat16)


def finish(rank, inputs, gain, incoming, grads, shares, block_rows):
    length, features = inputs.shape
    ranks = len(grads[0])
    flat = pl.BlockSpec((block_rows, features), lambda i, _: (i, 0))
    return pl.pallas_call(
        functools.partial(finish_kernel, shares, ranks),
        grid_spec=pltpu.PrefetchScalarGridSpec(
            num_scalar_prefetch=1,
            grid=(length // block_rows,),
            in_specs=[flat, pl.BlockSpec((1, features), lambda i, _: (0, 0))]
            + [pl.BlockSpec((ranks, block_rows, wide), lambda i, _: (0, i, 0)) for _, wide in shares]
            + [pl.BlockSpec((block_rows, wide), lambda i, _: (i, 0)) for _, wide in shares for _ in range(ranks)],
            out_specs=flat,
        ),
        out_shape=made(inputs.shape),
        compiler_params=params(16),
        cost_estimate=cost(12 * inputs.size, 8 * inputs.size),
    )(rank, inputs, gain, *incoming, *[x for part in grads for x in part])


def from_behind(x, axis, by):
    devices = lax.axis_size(axis)
    return lax.ppermute(x, axis, [(i, (i + by) % devices) for i in range(devices)])


def total(x, axis):
    passing, result = x, x
    for _ in range(lax.axis_size(axis) - 1):
        passing = from_behind(passing, axis, 1)
        result = result + passing
    return result


def after(values, events):
    return lax.optimization_barrier((tuple(values), tuple(events)))[0]


def swapped(pieces, earlier=None):
    devices = lax.axis_size("tensor")
    results = [pieces[0]]
    for k in range(1, devices):
        piece = after(pieces[k : k + 1], earlier[k : k + 1])[0] if earlier else pieces[k]
        results.append(lax.ppermute(piece, "tensor", [(i, i ^ k) for i in range(devices)]))
    return results


def body(upstream, inputs, keys, values, gain):
    ranks = lax.axis_size("tensor")
    tokens = inputs.shape[2]
    columns = keys.shape[3]
    shares = cut(columns, CHUNKS)

    upstream, inputs = upstream[0, 0], inputs[0, 0]
    keys, values = keys[0, 0], values[0, 0]
    rank = lax.axis_index("tensor")
    gain_columns = lax.dynamic_slice_in_dim(gain, rank * columns, columns, 1)
    rank = rank[None]

    handed, normed = prepare(rank, upstream, inputs, shares, ranks, min(64, tokens))

    latest = None
    for c, pieces in enumerate(normed):
        normed[c] = latest = swapped(pieces, latest)
    incoming = []
    for c, held in enumerate(handed):
        if c >= 2:
            (held,) = after([held], [incoming[c - 2]])
        incoming.append(from_behind(held, "pipe", -1))
    grad_out = []
    for held in incoming:
        latest = swapped([held] + [held[k] for k in range(1, ranks)], latest)
        grad_out.append(latest)

    grads, gain_parts, earlier = [], [], ()
    for c, share in enumerate(shares):
        if 0 < c < len(shares) - 1:
            grad_out[c] = list(after(grad_out[c], [incoming[c + 1]]))
        grad_queries, earlier, gain_part = attention_back(
            share, rank, normed[c], grad_out[c], keys, values, gain_columns, earlier
        )
        gain_parts.append(gain_part)
        grads.append(swapped(grad_queries, grads[-1] if grads else None))
    grad_keys, grad_values = earlier
    grad_gain = total(jnp.concatenate(gain_parts, axis=1), "dp")
    grad_inputs = finish(rank, inputs, gain, incoming, grads, shares, min(64, tokens))
    return (
        grad_inputs[None, None],
        grad_keys[None, None],
        grad_values[None, None],
        grad_gain,
    )


def solution(mesh):
    in_specs = (
        P("pipe", "dp", "tensor", None),
        P("pipe", "dp", "tensor", None),
        P("pipe", "dp", None, "tensor"),
        P("pipe", "dp", None, "tensor"),
        P("pipe", None),
    )
    out_specs = (
        P("pipe", "dp", "tensor", None),
        P("pipe", "dp", None, "tensor"),
        P("pipe", "dp", None, "tensor"),
        P("pipe", "tensor"),
    )
    return jax.shard_map(body, mesh=mesh, in_specs=in_specs, out_specs=out_specs, check_vma=False)
```

time: 843 us -> 130 us (0.15)
  matrix products: 285 us -> 0 us
  waiting for transfers between devices: 232 us -> 44.7 us
  local copies, waits for them, and re-layouts: 166 us -> 4.42 us
  other arithmetic: 111 us -> 0.6 us
  Pallas kernels: 0 us -> 47.2 us
  starting transfers between devices: 13.1 us -> 31.5 us
  loops' own time: 14.5 us -> 0 us
  between operations: 14.4 us -> 0.81 us
    dot_general x10 -> x0, matrix products: 285 us -> none  [the longest x2 108 us: block_step(): jnp.einsum('mhqk,mkhd->mqhd', grad_scores, key_heads, preferred_element_t...]
    ppermute x1 -> x4, waiting for transfers between devices: 123 us -> 12.9 us  [from_behind(): lax.ppermute(x, axis, [(i, (i + by) % devices) for i in range(devices)])]
    all_gather x1 -> x0, waiting for transfers between devices: 86.6 us -> none  [body(): full_rows = lax.all_gather(upstream, 'tensor', axis=2, tiled=True)]
    convert_element_type x5 -> x0, local copies, waits for them, and re-layouts: 71.3 us -> none  [the longest x1 37.2 us: body(): normed_b = normed.astype(jnp.bfloat16)]
    unnamed x4 -> x0, other arithmetic: 51.8 us -> none
    unnamed x31 -> x36, local copies, waits for them, and re-layouts: 54.1 us -> 4.26 us
    pallas_call x0 -> x5, Pallas kernels: none -> 47.2 us  [the longest x3 38 us: attention_back(): pl.pallas_call(functools.partial(attention_kernel, ranks), grid_spec=pltp...]
    reduce_sum x5 -> x0, other arithmetic: 36.6 us -> none  [the longest x2 23.6 us: block_step(): jnp.sum(jnp.exp(scores - row_max), axis=-1, keepdims=True)]
  transfers between devices with their start and end apart: 4 -> 31, of which waited for: 3 -> 12; matrix products, arithmetic and copies ran while one was open for 19% -> 1% of each run, Pallas kernels for 0% -> 29%
where the time goes in v1:
time: 130 us; the launch traced here: 129 us
  Pallas kernels  47.2 us (36%)
  waiting for transfers between devices  44.7 us (34%)
  starting transfers between devices  31.5 us (24%)
  local copies, waits for them, and re-layouts  4.42 us (3%)
    pallas_call x3, Pallas kernels, attention_back(): pl.pallas_call(functools.partial(attention_kernel, ranks), grid_spec=pltp...  38 us
    ppermute x27, waiting for transfers between devices, swapped(): lax.ppermute(piece, 'tensor', [(i, i ^ k) for i in range(devices)])  31.8 us
    ppermute x27, starting transfers between devices, swapped(): lax.ppermute(piece, 'tensor', [(i, i ^ k) for i in range(devices)])  23.9 us
    ppermute x4, waiting for transfers between devices, from_behind(): lax.ppermute(x, axis, [(i, (i + by) % devices) for i in range(devices)])  12.9 us
    ppermute x4, starting transfers between devices, from_behind(): lax.ppermute(x, axis, [(i, (i + by) % devices) for i in range(devices)])  7.6 us
    pallas_call x1, Pallas kernels, finish(): pl.pallas_call(functools.partial(finish_kernel, shares, ranks), grid_spec...  4.74 us
    pallas_call x1, Pallas kernels, prepare(): pl.pallas_call(functools.partial(prepare_kernel, shares, ranks, steps), g...  4.48 us
    unnamed x36, local copies, waits for them, and re-layouts  4.26 us
  transfers between devices with their start and end apart: 31, of which 12 were waited for; matrix products, arithmetic and copies ran while one was open for 1% of the time, Pallas kernels for 29%

profile of v1, /device:TPU:0, one launch (start us, length us, event | category | flops | bytes accessed | tf_op | source)
XLA Modules:
  0.0 129.2 jit_solution(7090630218823502909)
XLA Ops:
  0.6 4.5 %shard_map.84 = (bf16[4,256,512]{2,1,0:T(8,128)(2,1)}, bf16[4,256,512]{2,1,0:T(8,128)(2,1)}, bf16[4,256,512]{2,1,0:T(8,128)(2,1)S(1)}, bf16[256,512]{1,0:T(8,128...) custom-call(s32[1]{0:T(128)} %bitcast.rank_ref, ...), custom_call_target="tpu_custom_call" | custom-call | flops 6291456 | bytes 12582912 | tf_op jit(solution)/shard_map/pallas_call | solution.py:79
  5.1 5.1 %collective-permute-start = (bf16[4,256,512]{2,1,0:T(8,128)(2,1)}, bf16[4,256,512]{2,1,0:T(8,128)(2,1)S(1)}, u32[]{:S(2)}, u32[]{:S(2)}) collective-permute-start(bf16[4,256,512]{2,1,0:T(8,128)(2,1)} %get-tuple-element.66), channel_id=1, source_target_pairs={{0,12},{4,0},{8,4},{12,8},{1,13},{5,1},{9,5},{13,9},{2,14},{6,2},{... | collective-permute-start | bytes 3145736 | tf_op jit(solution)/shard_map/ppermute | solution.py:298
  10.7 1.5 %collective-permute-start.4 = (bf16[256,512]{1,0:T(8,128)(2,1)S(1)}, bf16[256,512]{1,0:T(8,128)(2,1)S(1)}, u32[]{:S(2)}, u32[]{:S(2)}) collective-permute-start(bf16[256,512]{1,0:T(8,128)(2,1)S(1)} %get-tuple-element.72), channel_id=1, source_target_pairs={{0,2},{1,3},{2,0},{3,1},{4,6},{5,7},{6,4},{7,5},{8,10},{9,11},{10,... | collective-permute-start | bytes 786440 | tf_op jit(solution)/shard_map/ppermute | solution.py:318
  13.5 6.3 %collective-permute-done.4.refs_2_ = bf16[256,512]{1,0:T(8,128)(2,1)S(1)} collective-permute-done((bf16[256,512]{1,0:T(8,128)(2,1)S(1)}, bf16[256,512]{1,0:T(8,128)(2,1)S(1)}, u32[]{:S(2)}, u32[]{:S(2)}) %collective-permute-start.4) | collective-permute-done | bytes 262176 | tf_op jit(solution)/shard_map/ppermute | solution.py:318
  20.5 1.5 %collective-permute-start.9 = (bf16[256,512]{1,0:T(8,128)(2,1)S(1)}, bf16[256,512]{1,0:T(8,128)(2,1)S(1)}, u32[]{:S(2)}, u32[]{:S(2)}) collective-permute-start(bf16[256,512]{1,0:T(8,128)(2,1)S(1)} %get-tuple-element.81), channel_id=1, source_target_pairs={{0,2},{1,3},{2,0},{3,1},{4,6},{5,7},{6,4},{7,5},{8,10},{9,11},{10,... | collective-permute-start | bytes 786440 | tf_op jit(solution)/shard_map/ppermute | solution.py:318
  22.0 2.6 %collective-permute-done.5.refs_3_ = bf16[256,512]{1,0:T(8,128)(2,1)S(1)} collective-permute-done((bf16[256,512]{1,0:T(8,128)(2,1)S(1)}, bf16[256,512]{1,0:T(8,128)(2,1)S(1)}, u32[]{:S(2)}, u32[]{:S(2)}) %collective-permute-start.5) | collective-permute-done | bytes 262176 | tf_op jit(solution)/shard_map/ppermute | solution.py:318
  25.3 2.0 %collective-permute-start.12 = (bf16[256,512]{1,0:T(8,128)(2,1)S(1)}, bf16[256,512]{1,0:T(8,128)(2,1)S(1)}, u32[]{:S(2)}, u32[]{:S(2)}) collective-permute-start(bf16[256,512]{1,0:T(8,128)(2,1)S(1)} %get-tuple-element.86), channel_id=1, source_target_pairs={{0,3},{1,2},{2,1},{3,0},{4,7},{5,6},{6,5},{7,4},{8,11},{9,10},{10,... | collective-permute-start | bytes 786440 | tf_op jit(solution)/shard_map/ppermute | solution.py:318
  28.1 3.0 %collective-permute-done.9.refs_2_ = bf16[256,512]{1,0:T(8,128)(2,1)S(1)} collective-permute-done((bf16[256,512]{1,0:T(8,128)(2,1)S(1)}, bf16[256,512]{1,0:T(8,128)(2,1)S(1)}, u32[]{:S(2)}, u32[]{:S(2)}) %collective-permute-start.9) | collective-permute-done | bytes 262176 | tf_op jit(solution)/shard_map/ppermute | solution.py:318
  31.8 1.5 %collective-permute-start.10 = (bf16[256,512]{1,0:T(8,128)(2,1)}, bf16[256,512]{1,0:T(8,128)(2,1)}, u32[]{:S(2)}, u32[]{:S(2)}) collective-permute-start(bf16[256,512]{1,0:T(8,128)(2,1)} %get-tuple-element.82), channel_id=1, source_target_pairs={{0,2},{1,3},{2,0},{3,1},{4,6},{5,7},{6,4},{7,5},{8,10},{9,11},{10,... | collective-permute-start | bytes 786440 | tf_op jit(solution)/shard_map/ppermute | solution.py:318
  33.3 2.6 %collective-permute-done.12.refs_3_ = bf16[256,512]{1,0:T(8,128)(2,1)S(1)} collective-permute-done((bf16[256,512]{1,0:T(8,128)(2,1)S(1)}, bf16[256,512]{1,0:T(8,128)(2,1)S(1)}, u32[]{:S(2)}, u32[]{:S(2)}) %collective-permute-start.12) | collective-permute-done | bytes 262176 | tf_op jit(solution)/shard_map/ppermute | solution.py:318
  36.6 2.0 %collective-permute-start.13 = (bf16[256,512]{1,0:T(8,128)(2,1)}, bf16[256,512]{1,0:T(8,128)(2,1)}, u32[]{:S(2)}, u32[]{:S(2)}) collective-permute-start(bf16[256,512]{1,0:T(8,128)(2,1)} %get-tuple-element.87), channel_id=1, source_target_pairs={{0,3},{1,2},{2,1},{3,0},{4,7},{5,6},{6,5},{7,4},{8,11},{9,10},{10,... | collective-permute-start | bytes 786440 | tf_op jit(solution)/shard_map/ppermute | solution.py:318
  39.2 3.1 %collective-permute-done.10.refs_2_ = bf16[256,512]{1,0:T(8,128)(2,1)} collective-permute-done((bf16[256,512]{1,0:T(8,128)(2,1)}, bf16[256,512]{1,0:T(8,128)(2,1)}, u32[]{:S(2)}, u32[]{:S(2)}) %collective-permute-start.10) | collective-permute-done | bytes 262176 | tf_op jit(solution)/shard_map/ppermute | solution.py:318
  42.4 1.5 %collective-permute-start.11 = (bf16[256,512]{1,0:T(8,128)(2,1)S(1)}, bf16[256,512]{1,0:T(8,128)(2,1)S(1)}, u32[]{:S(2)}, u32[]{:S(2)}) collective-permute-start(bf16[256,512]{1,0:T(8,128)(2,1)S(1)} %get-tuple-element.83), channel_id=1, source_target_pairs={{0,2},{1,3},{2,0},{3,1},{4,6},{5,7},{6,4},{7,5},{8,10},{9,11},{10,... | collective-permute-start | bytes 786440 | tf_op jit(solution)/shard_map/ppermute | solution.py:318
  43.9 3.3 %collective-permute-done.13.refs_3_ = bf16[256,512]{1,0:T(8,128)(2,1)} collective-permute-done((bf16[256,512]{1,0:T(8,128)(2,1)}, bf16[256,512]{1,0:T(8,128)(2,1)}, u32[]{:S(2)}, u32[]{:S(2)}) %collective-permute-start.13) | collective-permute-done | bytes 262176 | tf_op jit(solution)/shard_map/ppermute | solution.py:318
  47.2 1.9 %collective-permute-start.14 = (bf16[256,512]{1,0:T(8,128)(2,1)S(1)}, bf16[256,512]{1,0:T(8,128)(2,1)S(1)}, u32[]{:S(2)}, u32[]{:S(2)}) collective-permute-start(bf16[256,512]{1,0:T(8,128)(2,1)S(1)} %get-tuple-element.88), channel_id=1, source_target_pairs={{0,3},{1,2},{2,1},{3,0},{4,7},{5,6},{6,5},{7,4},{8,11},{9,10},{10,... | collective-permute-start | bytes 786440 | tf_op jit(solution)/shard_map/ppermute | solution.py:318
  49.1 7.5 %collective-permute-done.1.refs_4_.refs_1_ = bf16[4,256,512]{2,1,0:T(8,128)(2,1)S(1)} collective-permute-done((bf16[4,256,512]{2,1,0:T(8,128)(2,1)}, bf16[4,256,512]{2,1,0:T(8,128)(2,1)S(1)}, u32[]{:S(2)}, u32[]{:S(2)}) %collective-permute-start.1) | collective-permute-done | bytes 1048608 | tf_op jit(solution)/shard_map/ppermute | solution.py:298
  56.7 1.6 %collective-permute-start.19 = (bf16[256,512]{1,0:T(8,128)(2,1)S(1)}, bf16[256,512]{1,0:T(8,128)(2,1)S(1)}, u32[]{:S(2)}, u32[]{:S(2)}) collective-permute-start(bf16[256,512]{1,0:T(8,128)(2,1)S(1)} %get-tuple-element.95), channel_id=1, source_target_pairs={{0,2},{1,3},{2,0},{3,1},{4,6},{5,7},{6,4},{7,5},{8,10},{9,11},{10,... | collective-permute-start | bytes 786440 | tf_op jit(solution)/shard_map/ppermute | solution.py:318
  58.3 1.6 %collective-permute-start.20 = (bf16[256,512]{1,0:T(8,128)(2,1)S(1)}, bf16[256,512]{1,0:T(8,128)(2,1)S(1)}, u32[]{:S(2)}, u32[]{:S(2)}) collective-permute-start(bf16[256,512]{1,0:T(8,128)(2,1)S(1)} %get-tuple-element.96), channel_id=1, source_target_pairs={{0,3},{1,2},{2,1},{3,0},{4,7},{5,6},{6,5},{7,4},{8,11},{9,10},{10,... | collective-permute-start | bytes 786440 | tf_op jit(solution)/shard_map/ppermute | solution.py:318
  60.0 12.6 %shard_map.85 = (bf16[256,512]{1,0:T(8,128)(2,1)S(1)}, bf16[256,512]{1,0:T(8,128)(2,1)S(1)}, bf16[256,512]{1,0:T(8,128)(2,1)S(1)}, bf16[256,512]{1,0:T(8,128)(2,...) custom-call(s32[1]{0:T(128)} %bitcast.rank_ref, ...), custom_call_target="tpu_custom_call" | custom-call | flops 5368709120 | bytes 33554432 | tf_op jit(solution)/shard_map/pallas_call | solution.py:222
  73.2 1.3 collective-permute-start.17
  74.5 3.3 %collective-permute-done.2.refs_4_.refs_2_ = bf16[4,256,512]{2,1,0:T(8,128)(2,1)S(1)} collective-permute-done((bf16[4,256,512]{2,1,0:T(8,128)(2,1)S(1)}, bf16[4,256,512]{2,1,0:T(8,128)(2,1)S(1)}, u32[]{:S(2)}, u32[]{:S(2)}) %collective-permute-start.2) | collective-permute-done | bytes 1048608 | tf_op jit(solution)/shard_map/ppermute | solution.py:298
  77.9 1.6 %collective-permute-start.25 = (bf16[256,512]{1,0:T(8,128)(2,1)S(1)}, bf16[256,512]{1,0:T(8,128)(2,1)S(1)}, u32[]{:S(2)}, u32[]{:S(2)}) collective-permute-start(bf16[256,512]{1,0:T(8,128)(2,1)S(1)} %get-tuple-element.112), channel_id=1, source_target_pairs={{0,2},{1,3},{2,0},{3,1},{4,6},{5,7},{6,4},{7,5},{8,10},{9,11},{10,... | collective-permute-start | bytes 786440 | tf_op jit(solution)/shard_map/ppermute | solution.py:318
  79.8 12.5 %shard_map.86 = (bf16[256,512]{1,0:T(8,128)(2,1)S(1)}, bf16[256,512]{1,0:T(8,128)(2,1)S(1)}, bf16[256,512]{1,0:T(8,128)(2,1)S(1)}, bf16[256,512]{1,0:T(8,128)(2,...) custom-call(s32[1]{0:T(128)} %bitcast.rank_ref, ...), custom_call_target="tpu_custom_call", output_to_operand_aliasing={{4}: (12, {}), {5}: (13, {})} | custom-call | flops 5368709120 | bytes 33554432 | tf_op jit(solution)/shard_map/pallas_call | solution.py:222
  92.7 1.5 %collective-permute-start.22 = (bf16[256,512]{1,0:T(8,128)(2,1)S(1)}, bf16[256,512]{1,0:T(8,128)(2,1)S(1)}, u32[]{:S(2)}, u32[]{:S(2)}) collective-permute-start(bf16[256,512]{1,0:T(8,128)(2,1)S(1)} %get-tuple-element.107), channel_id=1, source_target_pairs={{0,2},{1,3},{2,0},{3,1},{4,6},{5,7},{6,4},{7,5},{8,10},{9,11},{10,... | collective-permute-start | bytes 786440 | tf_op jit(solution)/shard_map/ppermute | solution.py:318
  94.2 3.5 %collective-permute-done.26.refs_7_ = bf16[256,512]{1,0:T(8,128)(2,1)S(1)} collective-permute-done((bf16[256,512]{1,0:T(8,128)(2,1)S(1)}, bf16[256,512]{1,0:T(8,128)(2,1)S(1)}, u32[]{:S(2)}, u32[]{:S(2)}) %collective-permute-start.26) | collective-permute-done | bytes 262176 | tf_op jit(solution)/shard_map/ppermute | solution.py:318
  97.8 12.8 %shard_map.87 = (bf16[256,512]{1,0:T(8,128)(2,1)S(1)}, bf16[256,512]{1,0:T(8,128)(2,1)S(1)}, bf16[256,512]{1,0:T(8,128)(2,1)S(1)}, bf16[256,512]{1,0:T(8,128)(2,...) custom-call(s32[1]{0:T(128)} %bitcast.rank_ref, ...), custom_call_target="tpu_custom_call", output_to_operand_aliasing={{4}: (12, {}), {5}: (13, {})} | custom-call | flops 5368709120 | bytes 33554432 | tf_op jit(solution)/shard_map/pallas_call | solution.py:222
  111.9 0.9 collective-permute-start.29
  112.9 1.5 %collective-permute-start.30 = (f32[1,1536]{1,0:T(1,128)S(1)}, f32[1,1536]{1,0:T(1,128)S(1)}, u32[]{:S(2)}, u32[]{:S(2)}) collective-permute-start(f32[1,1536]{1,0:T(1,128)S(1)} %constant_dynamic-update-slice_fusion), channel_id=1, source_target_pairs={{0,16},{16,0},{1,17},{17,1},{2,18},{18,2},{3,19},{19,3},{4,20},{20... | collective-permute-start | bytes 18440 | tf_op jit(solution)/shard_map/ppermute | solution.py:298
  114.4 2.1 %collective-permute-done.30 = f32[1,1536]{1,0:T(1,128)S(1)} collective-permute-done((f32[1,1536]{1,0:T(1,128)S(1)}, f32[1,1536]{1,0:T(1,128)S(1)}, u32[]{:S(2)}, u32[]{:S(2)}) %collective-permute-start.30) | collective-permute-done | bytes 6176 | tf_op jit(solution)/shard_map/ppermute | solution.py:298
  117.2 3.4 %collective-permute-done.28.refs_13_ = bf16[256,512]{1,0:T(8,128)(2,1)S(1)} collective-permute-done((bf16[256,512]{1,0:T(8,128)(2,1)S(1)}, bf16[256,512]{1,0:T(8,128)(2,1)S(1)}, u32[]{:S(2)}, u32[]{:S(2)}) %collective-permute-start.28) | collective-permute-done | bytes 262176 | tf_op jit(solution)/shard_map/ppermute | solution.py:318
  120.6 3.9 %collective-permute-done.29.refs_14_ = bf16[256,512]{1,0:T(8,128)(2,1)S(1)} collective-permute-done((bf16[256,512]{1,0:T(8,128)(2,1)S(1)}, bf16[256,512]{1,0:T(8,128)(2,1)S(1)}, u32[]{:S(2)}, u32[]{:S(2)}) %collective-permute-start.29) | collective-permute-done | bytes 262176 | tf_op jit(solution)/shard_map/ppermute | solution.py:318
  124.5 4.7 %shard_map.88 = bf16[256,6144]{1,0:T(8,128)(2,1)} custom-call(s32[1]{0:T(128)} %bitcast.rank_ref, bf16[256,6144]{1,0:T(8,128)(2,1)S(1)} %bitcast.27, f32[1,6144]{1,0:T(1,128)S(1)} %copy-done.1, bf16[4,256,512]{2,1,0:T(8,128)(2,1)S(1)} %collective-permute-done.refs_4_.refs_0_, bf16[4,256,512]{2,1,0:T(8,128)(2,1)S(1)} %collective-permute-done.1.refs_4_.refs_1_, ...), custom_call_target="tpu_custom_call" | custom-call | flops 18874368 | bytes 12582912 | tf_op jit(solution)/shard_map/pallas_call | solution.py:280
  (77 shorter events, 9.4 us)
Async XLA Ops:
  0.6 48.5 %copy-start.1 = (f32[1,6144]{1,0:T(1,128)S(1)}, f32[1,6144]{1,0:T(1,128)}, u32[]{:S(2)}) copy-start(f32[1,6144]{1,0:T(1,128)} %gain_ref.1) | copy-start | bytes 73732
  5.1 33.5 %collective-permute-start = (bf16[4,256,512]{2,1,0:T(8,128)(2,1)}, bf16[4,256,512]{2,1,0:T(8,128)(2,1)S(1)}, u32[]{:S(2)}, u32[]{:S(2)}) collective-permute-start(bf16[4,256,512]{2,1,0:T(8,128)(2,1)} %get-tuple-element.66), channel_id=1, source_target_pairs={{0,12},{4,0},{8,4},{12,8},{1,13},{5,1},{9,5},{13,9},{2,14},{6,2},{... | collective-permute-start | bytes 3145736 | tf_op jit(solution)/shard_map/ppermute | solution.py:298
  10.2 46.4 %collective-permute-start.1 = (bf16[4,256,512]{2,1,0:T(8,128)(2,1)}, bf16[4,256,512]{2,1,0:T(8,128)(2,1)S(1)}, u32[]{:S(2)}, u32[]{:S(2)}) collective-permute-start(bf16[4,256,512]{2,1,0:T(8,128)(2,1)} %get-tuple-element.67), channel_id=1, source_target_pairs={{0,12},{4,0},{8,4},{12,8},{1,13},{5,1},{9,5},{13,9},{2,14},{6,2},{... | collective-permute-start | bytes 3145736 | tf_op jit(solution)/shard_map/ppermute | solution.py:298
  10.7 1.9 %collective-permute-start.3 = (bf16[256,512]{1,0:T(8,128)(2,1)S(1)}, bf16[256,512]{1,0:T(8,128)(2,1)S(1)}, u32[]{:S(2)}, u32[]{:S(2)}) collective-permute-start(bf16[256,512]{1,0:T(8,128)(2,1)S(1)} %get-tuple-element.71), channel_id=1, source_target_pairs={{0,1},{1,0},{2,3},{3,2},{4,5},{5,4},{6,7},{7,6},{8,9},{9,8},{10,11... | collective-permute-start | bytes 786440 | tf_op jit(solution)/shard_map/ppermute | solution.py:318
  10.7 9.1 %collective-permute-start.4 = (bf16[256,512]{1,0:T(8,128)(2,1)S(1)}, bf16[256,512]{1,0:T(8,128)(2,1)S(1)}, u32[]{:S(2)}, u32[]{:S(2)}) collective-permute-start(bf16[256,512]{1,0:T(8,128)(2,1)S(1)} %get-tuple-element.72), channel_id=1, source_target_pairs={{0,2},{1,3},{2,0},{3,1},{4,6},{5,7},{6,4},{7,5},{8,10},{9,11},{10,... | collective-permute-start | bytes 786440 | tf_op jit(solution)/shard_map/ppermute | solution.py:318
  12.2 12.4 %collective-permute-start.5 = (bf16[256,512]{1,0:T(8,128)(2,1)S(1)}, bf16[256,512]{1,0:T(8,128)(2,1)S(1)}, u32[]{:S(2)}, u32[]{:S(2)}) collective-permute-start(bf16[256,512]{1,0:T(8,128)(2,1)S(1)} %get-tuple-element.73), channel_id=1, source_target_pairs={{0,3},{1,2},{2,1},{3,0},{4,7},{5,6},{6,5},{7,4},{8,11},{9,10},{10,... | collective-permute-start | bytes 786440 | tf_op jit(solution)/shard_map/ppermute | solution.py:318
  13.3 14.1 %collective-permute-start.6 = (bf16[256,512]{1,0:T(8,128)(2,1)S(1)}, bf16[256,512]{1,0:T(8,128)(2,1)S(1)}, u32[]{:S(2)}, u32[]{:S(2)}) collective-permute-start(bf16[256,512]{1,0:T(8,128)(2,1)S(1)} %get-tuple-element.76), channel_id=1, source_target_pairs={{0,1},{1,0},{2,3},{3,2},{4,5},{5,4},{6,7},{7,6},{8,9},{9,8},{10,11... | collective-permute-start | bytes 786440 | tf_op jit(solution)/shard_map/ppermute | solution.py:318
  20.5 10.5 %collective-permute-start.9 = (bf16[256,512]{1,0:T(8,128)(2,1)S(1)}, bf16[256,512]{1,0:T(8,128)(2,1)S(1)}, u32[]{:S(2)}, u32[]{:S(2)}) collective-permute-start(bf16[256,512]{1,0:T(8,128)(2,1)S(1)} %get-tuple-element.81), channel_id=1, source_target_pairs={{0,2},{1,3},{2,0},{3,1},{4,6},{5,7},{6,4},{7,5},{8,10},{9,11},{10,... | collective-permute-start | bytes 786440 | tf_op jit(solution)/shard_map/ppermute | solution.py:318
  25.3 10.5 %collective-permute-start.12 = (bf16[256,512]{1,0:T(8,128)(2,1)S(1)}, bf16[256,512]{1,0:T(8,128)(2,1)S(1)}, u32[]{:S(2)}, u32[]{:S(2)}) collective-permute-start(bf16[256,512]{1,0:T(8,128)(2,1)S(1)} %get-tuple-element.86), channel_id=1, source_target_pairs={{0,3},{1,2},{2,1},{3,0},{4,7},{5,6},{6,5},{7,4},{8,11},{9,10},{10,... | collective-permute-start | bytes 786440 | tf_op jit(solution)/shard_map/ppermute | solution.py:318
  28.1 11.1 %collective-permute-start.7 = (bf16[256,512]{1,0:T(8,128)(2,1)}, bf16[256,512]{1,0:T(8,128)(2,1)S(1)}, u32[]{:S(2)}, u32[]{:S(2)}) collective-permute-start(bf16[256,512]{1,0:T(8,128)(2,1)} %get-tuple-element.77), channel_id=1, source_target_pairs={{0,1},{1,0},{2,3},{3,2},{4,5},{5,4},{6,7},{7,6},{8,9},{9,8},{10,11... | collective-permute-start | bytes 786440 | tf_op jit(solution)/shard_map/ppermute | solution.py:318
  31.8 10.6 %collective-permute-start.10 = (bf16[256,512]{1,0:T(8,128)(2,1)}, bf16[256,512]{1,0:T(8,128)(2,1)}, u32[]{:S(2)}, u32[]{:S(2)}) collective-permute-start(bf16[256,512]{1,0:T(8,128)(2,1)} %get-tuple-element.82), channel_id=1, source_target_pairs={{0,2},{1,3},{2,0},{3,1},{4,6},{5,7},{6,4},{7,5},{8,10},{9,11},{10,... | collective-permute-start | bytes 786440 | tf_op jit(solution)/shard_map/ppermute | solution.py:318
  36.6 10.6 %collective-permute-start.13 = (bf16[256,512]{1,0:T(8,128)(2,1)}, bf16[256,512]{1,0:T(8,128)(2,1)}, u32[]{:S(2)}, u32[]{:S(2)}) collective-permute-start(bf16[256,512]{1,0:T(8,128)(2,1)} %get-tuple-element.87), channel_id=1, source_target_pairs={{0,3},{1,2},{2,1},{3,0},{4,7},{5,6},{6,5},{7,4},{8,11},{9,10},{10,... | collective-permute-start | bytes 786440 | tf_op jit(solution)/shard_map/ppermute | solution.py:318
  38.6 39.2 %collective-permute-start.2 = (bf16[4,256,512]{2,1,0:T(8,128)(2,1)S(1)}, bf16[4,256,512]{2,1,0:T(8,128)(2,1)S(1)}, u32[]{:S(2)}, u32[]{:S(2)}) collective-permute-start(bf16[4,256,512]{2,1,0:T(8,128)(2,1)S(1)} %get-tuple-element.69), channel_id=1, source_target_pairs={{0,12},{4,0},{8,4},{12,8},{1,13},{5,1},{9,5},{13,9},{2,14},{6,2},{... | collective-permute-start | bytes 3145736 | tf_op jit(solution)/shard_map/ppermute | solution.py:298
  39.2 17.5 %collective-permute-start.8 = (bf16[256,512]{1,0:T(8,128)(2,1)S(1)}, bf16[256,512]{1,0:T(8,128)(2,1)S(1)}, u32[]{:S(2)}, u32[]{:S(2)}) collective-permute-start(bf16[256,512]{1,0:T(8,128)(2,1)S(1)} %get-tuple-element.78), channel_id=1, source_target_pairs={{0,1},{1,0},{2,3},{3,2},{4,5},{5,4},{6,7},{7,6},{8,9},{9,8},{10,11... | collective-permute-start | bytes 786440 | tf_op jit(solution)/shard_map/ppermute | solution.py:318
  42.4 14.4 %collective-permute-start.11 = (bf16[256,512]{1,0:T(8,128)(2,1)S(1)}, bf16[256,512]{1,0:T(8,128)(2,1)S(1)}, u32[]{:S(2)}, u32[]{:S(2)}) collective-permute-start(bf16[256,512]{1,0:T(8,128)(2,1)S(1)} %get-tuple-element.83), channel_id=1, source_target_pairs={{0,2},{1,3},{2,0},{3,1},{4,6},{5,7},{6,4},{7,5},{8,10},{9,11},{10,... | collective-permute-start | bytes 786440 | tf_op jit(solution)/shard_map/ppermute | solution.py:318
  47.2 11.1 %collective-permute-start.14 = (bf16[256,512]{1,0:T(8,128)(2,1)S(1)}, bf16[256,512]{1,0:T(8,128)(2,1)S(1)}, u32[]{:S(2)}, u32[]{:S(2)}) collective-permute-start(bf16[256,512]{1,0:T(8,128)(2,1)S(1)} %get-tuple-element.88), channel_id=1, source_target_pairs={{0,3},{1,2},{2,1},{3,0},{4,7},{5,6},{6,5},{7,4},{8,11},{9,10},{10,... | collective-permute-start | bytes 786440 | tf_op jit(solution)/shard_map/ppermute | solution.py:318
  56.7 16.0 %collective-permute-start.18 = (bf16[256,512]{1,0:T(8,128)(2,1)S(1)}, bf16[256,512]{1,0:T(8,128)(2,1)S(1)}, u32[]{:S(2)}, u32[]{:S(2)}) collective-permute-start(bf16[256,512]{1,0:T(8,128)(2,1)S(1)} %get-tuple-element.94), channel_id=1, source_target_pairs={{0,1},{1,0},{2,3},{3,2},{4,5},{5,4},{6,7},{7,6},{8,9},{9,8},{10,11... | collective-permute-start | bytes 786440 | tf_op jit(solution)/shard_map/ppermute | solution.py:318
  56.7 16.5 %collective-permute-start.19 = (bf16[256,512]{1,0:T(8,128)(2,1)S(1)}, bf16[256,512]{1,0:T(8,128)(2,1)S(1)}, u32[]{:S(2)}, u32[]{:S(2)}) collective-permute-start(bf16[256,512]{1,0:T(8,128)(2,1)S(1)} %get-tuple-element.95), channel_id=1, source_target_pairs={{0,2},{1,3},{2,0},{3,1},{4,6},{5,7},{6,4},{7,5},{8,10},{9,11},{10,... | collective-permute-start | bytes 786440 | tf_op jit(solution)/shard_map/ppermute | solution.py:318
  58.3 16.2 %collective-permute-start.20 = (bf16[256,512]{1,0:T(8,128)(2,1)S(1)}, bf16[256,512]{1,0:T(8,128)(2,1)S(1)}, u32[]{:S(2)}, u32[]{:S(2)}) collective-permute-start(bf16[256,512]{1,0:T(8,128)(2,1)S(1)} %get-tuple-element.96), channel_id=1, source_target_pairs={{0,3},{1,2},{2,1},{3,0},{4,7},{5,6},{6,5},{7,4},{8,11},{9,10},{10,... | collective-permute-start | bytes 786440 | tf_op jit(solution)/shard_map/ppermute | solution.py:318
  72.7 6.9 %collective-permute-start.15 = (bf16[256,512]{1,0:T(8,128)(2,1)S(1)}, bf16[256,512]{1,0:T(8,128)(2,1)S(1)}, u32[]{:S(2)}, u32[]{:S(2)}) collective-permute-start(bf16[256,512]{1,0:T(8,128)(2,1)S(1)} %get-tuple-element.90), channel_id=1, source_target_pairs={{0,1},{1,0},{2,3},{3,2},{4,5},{5,4},{6,7},{7,6},{8,9},{9,8},{10,11... | collective-permute-start | bytes 786440 | tf_op jit(solution)/shard_map/ppermute | solution.py:318
  72.7 19.7 %collective-permute-start.16 = (bf16[256,512]{1,0:T(8,128)(2,1)S(1)}, bf16[256,512]{1,0:T(8,128)(2,1)S(1)}, u32[]{:S(2)}, u32[]{:S(2)}) collective-permute-start(bf16[256,512]{1,0:T(8,128)(2,1)S(1)} %get-tuple-element.91), channel_id=1, source_target_pairs={{0,2},{1,3},{2,0},{3,1},{4,6},{5,7},{6,4},{7,5},{8,10},{9,11},{10,... | collective-permute-start | bytes 786440 | tf_op jit(solution)/shard_map/ppermute | solution.py:318
  73.2 19.5 %collective-permute-start.17 = (bf16[256,512]{1,0:T(8,128)(2,1)S(1)}, bf16[256,512]{1,0:T(8,128)(2,1)S(1)}, u32[]{:S(2)}, u32[]{:S(2)}) collective-permute-start(bf16[256,512]{1,0:T(8,128)(2,1)S(1)} %get-tuple-element.92), channel_id=1, source_target_pairs={{0,3},{1,2},{2,1},{3,0},{4,7},{5,6},{6,5},{7,4},{8,11},{9,10},{10,... | collective-permute-start | bytes 786440 | tf_op jit(solution)/shard_map/ppermute | solution.py:318
  77.9 16.3 %collective-permute-start.24 = (bf16[256,512]{1,0:T(8,128)(2,1)S(1)}, bf16[256,512]{1,0:T(8,128)(2,1)S(1)}, u32[]{:S(2)}, u32[]{:S(2)}) collective-permute-start(bf16[256,512]{1,0:T(8,128)(2,1)S(1)} %get-tuple-element.111), channel_id=1, source_target_pairs={{0,1},{1,0},{2,3},{3,2},{4,5},{5,4},{6,7},{7,6},{8,9},{9,8},{10,11... | collective-permute-start | bytes 786440 | tf_op jit(solution)/shard_map/ppermute | solution.py:318
  77.9 16.3 %collective-permute-start.25 = (bf16[256,512]{1,0:T(8,128)(2,1)S(1)}, bf16[256,512]{1,0:T(8,128)(2,1)S(1)}, u32[]{:S(2)}, u32[]{:S(2)}) collective-permute-start(bf16[256,512]{1,0:T(8,128)(2,1)S(1)} %get-tuple-element.112), channel_id=1, source_target_pairs={{0,2},{1,3},{2,0},{3,1},{4,6},{5,7},{6,4},{7,5},{8,10},{9,11},{10,... | collective-permute-start | bytes 786440 | tf_op jit(solution)/shard_map/ppermute | solution.py:318
  79.5 18.2 %collective-permute-start.26 = (bf16[256,512]{1,0:T(8,128)(2,1)S(1)}, bf16[256,512]{1,0:T(8,128)(2,1)S(1)}, u32[]{:S(2)}, u32[]{:S(2)}) collective-permute-start(bf16[256,512]{1,0:T(8,128)(2,1)S(1)} %get-tuple-element.113), channel_id=1, source_target_pairs={{0,3},{1,2},{2,1},{3,0},{4,7},{5,6},{6,5},{7,4},{8,11},{9,10},{10,... | collective-permute-start | bytes 786440 | tf_op jit(solution)/shard_map/ppermute | solution.py:318
  92.3 18.3 %collective-permute-start.21 = (bf16[256,512]{1,0:T(8,128)(2,1)S(1)}, bf16[256,512]{1,0:T(8,128)(2,1)S(1)}, u32[]{:S(2)}, u32[]{:S(2)}) collective-permute-start(bf16[256,512]{1,0:T(8,128)(2,1)S(1)} %get-tuple-element.105), channel_id=1, source_target_pairs={{0,1},{1,0},{2,3},{3,2},{4,5},{5,4},{6,7},{7,6},{8,9},{9,8},{10,11... | collective-permute-start | bytes 786440 | tf_op jit(solution)/shard_map/ppermute | solution.py:318
  92.7 18.7 %collective-permute-start.22 = (bf16[256,512]{1,0:T(8,128)(2,1)S(1)}, bf16[256,512]{1,0:T(8,128)(2,1)S(1)}, u32[]{:S(2)}, u32[]{:S(2)}) collective-permute-start(bf16[256,512]{1,0:T(8,128)(2,1)S(1)} %get-tuple-element.107), channel_id=1, source_target_pairs={{0,2},{1,3},{2,0},{3,1},{4,6},{5,7},{6,4},{7,5},{8,10},{9,11},{10,... | collective-permute-start | bytes 786440 | tf_op jit(solution)/shard_map/ppermute | solution.py:318
  94.2 17.7 %collective-permute-start.23 = (bf16[256,512]{1,0:T(8,128)(2,1)S(1)}, bf16[256,512]{1,0:T(8,128)(2,1)S(1)}, u32[]{:S(2)}, u32[]{:S(2)}) collective-permute-start(bf16[256,512]{1,0:T(8,128)(2,1)S(1)} %get-tuple-element.109), channel_id=1, source_target_pairs={{0,3},{1,2},{2,1},{3,0},{4,7},{5,6},{6,5},{7,4},{8,11},{9,10},{10,... | collective-permute-start | bytes 786440 | tf_op jit(solution)/shard_map/ppermute | solution.py:318
  110.6 6.6 %collective-permute-start.27 = (bf16[256,512]{1,0:T(8,128)(2,1)S(1)}, bf16[256,512]{1,0:T(8,128)(2,1)S(1)}, u32[]{:S(2)}, u32[]{:S(2)}) collective-permute-start(bf16[256,512]{1,0:T(8,128)(2,1)S(1)} %get-tuple-element.118), channel_id=1, source_target_pairs={{0,1},{1,0},{2,3},{3,2},{4,5},{5,4},{6,7},{7,6},{8,9},{9,8},{10,11... | collective-permute-start | bytes 786440 | tf_op jit(solution)/shard_map/ppermute | solution.py:318
  111.4 9.2 %collective-permute-start.28 = (bf16[256,512]{1,0:T(8,128)(2,1)S(1)}, bf16[256,512]{1,0:T(8,128)(2,1)S(1)}, u32[]{:S(2)}, u32[]{:S(2)}) collective-permute-start(bf16[256,512]{1,0:T(8,128)(2,1)S(1)} %get-tuple-element.120), channel_id=1, source_target_pairs={{0,2},{1,3},{2,0},{3,1},{4,6},{5,7},{6,4},{7,5},{8,10},{9,11},{10,... | collective-permute-start | bytes 786440 | tf_op jit(solution)/shard_map/ppermute | solution.py:318
  111.9 12.5 %collective-permute-start.29 = (bf16[256,512]{1,0:T(8,128)(2,1)S(1)}, bf16[256,512]{1,0:T(8,128)(2,1)S(1)}, u32[]{:S(2)}, u32[]{:S(2)}) collective-permute-start(bf16[256,512]{1,0:T(8,128)(2,1)S(1)} %get-tuple-element.122), channel_id=1, source_target_pairs={{0,3},{1,2},{2,1},{3,0},{4,7},{5,6},{6,5},{7,4},{8,11},{9,10},{10,... | collective-permute-start | bytes 786440 | tf_op jit(solution)/shard_map/ppermute | solution.py:318
  112.9 3.7 %collective-permute-start.30 = (f32[1,1536]{1,0:T(1,128)S(1)}, f32[1,1536]{1,0:T(1,128)S(1)}, u32[]{:S(2)}, u32[]{:S(2)}) collective-permute-start(f32[1,1536]{1,0:T(1,128)S(1)} %constant_dynamic-update-slice_fusion), channel_id=1, source_target_pairs={{0,16},{16,0},{1,17},{17,1},{2,18},{18,2},{3,19},{19,3},{4,20},{20... | collective-permute-start | bytes 18440 | tf_op jit(solution)/shard_map/ppermute | solution.py:298
  (16 other events, 213.7 us)

commit v2 on v1

v2 whole, which is shorter than its diff:
```python
import functools
import math

import jax
import jax.numpy as jnp
from jax import lax
from jax.experimental import pallas as pl
from jax.experimental.pallas import tpu as pltpu
from jax.sharding import PartitionSpec as P

HEAD_DIM = 128
EPSILON = 1e-05
PARTS = (4, 9, 12)
BLOCK = 256
HEADS_A_STEP = 1
MIB = 1 << 20


def params(limit):
    return pltpu.CompilerParams(vmem_limit_bytes=limit * MIB)


def cost(flops, moved, exps=0):
    return pl.CostEstimate(flops=flops, bytes_accessed=moved, transcendentals=exps)


def made(shape, dtype=jnp.bfloat16):
    return jax.ShapeDtypeStruct(shape, dtype)


def cut(columns):
    heads = columns // HEAD_DIM
    bounds = [0] + [heads * part // PARTS[-1] * HEAD_DIM for part in PARTS]
    return [(start, end - start) for start, end in zip(bounds, bounds[1:]) if end > start]


def pinned(x):
    return pltpu.with_memory_space_constraint(x, pltpu.HBM)


def lead_kernel(share, ranks, rank_ref, upstream_ref, out_ref, arrived):
    start, wide = share
    columns = upstream_ref.shape[1] // ranks
    copies = []
    for k in range(ranks):
        at = pl.ds(pl.multiple_of((rank_ref[0] ^ k) * columns + start, HEAD_DIM), wide)
        copies.append(pltpu.make_async_copy(upstream_ref.at[:, at], out_ref.at[k], arrived.at[k]))
    for copy in copies:
        copy.start()
    for copy in copies:
        copy.wait()


def lead(rank, upstream, share, ranks):
    whole = pl.BlockSpec(memory_space=pl.ANY)
    return pl.pallas_call(
        functools.partial(lead_kernel, share, ranks),
        grid_spec=pltpu.PrefetchScalarGridSpec(
            num_scalar_prefetch=1,
            grid=(1,),
            in_specs=[whole],
            out_specs=whole,
            scratch_shapes=[pltpu.SemaphoreType.DMA((ranks,))],
        ),
        out_shape=made((ranks, upstream.shape[0], share[1])),
        compiler_params=params(4),
        cost_estimate=cost(0, upstream.size),
    )(rank, pinned(upstream))


def prepare_kernel(shares, ranks, steps, rank_ref, upstream_ref, inputs_ref, *refs):
    *out_refs, upstream_held, inputs_held, arrived = refs
    handed_refs, normed_refs = [None, *out_refs[: len(shares) - 1]], out_refs[len(shares) - 1 :]
    block_rows = inputs_ref.shape[0] // steps
    columns = inputs_ref.shape[1] // ranks
    step = pl.program_id(0)

    def copies(i):
        down = pl.ds(pl.multiple_of(i * block_rows, block_rows), block_rows)
        return [
            pltpu.make_async_copy(source.at[down, :], held.at[down, :], arrived.at[n, i])
            for n, (source, held) in enumerate(((inputs_ref, inputs_held), (upstream_ref, upstream_held)))
        ]

    @pl.when(step == 0)
    def _():
        for n in range(2):
            for i in range(steps):
                copies(i)[n].start()

    inputs_copy, upstream_copy = copies(step)
    inputs_copy.wait()
    down = pl.ds(pl.multiple_of(step * block_rows, block_rows), block_rows)
    x = inputs_held[down, :].astype(jnp.float32)
    inverse = 1.0 / jnp.sqrt(jnp.mean(x * x, axis=-1, keepdims=True) + EPSILON)
    for c, (start, wide) in enumerate(shares):
        for k in range(ranks):
            at = pl.ds(pl.multiple_of((rank_ref[0] ^ k) * columns + start, HEAD_DIM), wide)
            piece = inputs_held[down, at].astype(jnp.float32)
            normed_refs[c * ranks + k][...] = (piece * inverse).astype(jnp.bfloat16)
    upstream_copy.wait()
    for c, (start, wide) in list(enumerate(shares))[1:]:
        for k in range(ranks):
            at = pl.ds(pl.multiple_of((rank_ref[0] ^ k) * columns + start, HEAD_DIM), wide)
            handed_refs[c][k] = upstream_held[down, at]


def prepare(rank, upstream, inputs, shares, ranks, block_rows):
    length, features = inputs.shape
    steps = length // block_rows
    whole = pl.BlockSpec(memory_space=pl.ANY)

    def result(shape, near):
        return made(shape) if near else pltpu.HBM(shape, jnp.bfloat16)

    outs = pl.pallas_call(
        functools.partial(prepare_kernel, shares, ranks, steps),
        grid_spec=pltpu.PrefetchScalarGridSpec(
            num_scalar_prefetch=1,
            grid=(steps,),
            in_specs=[whole, whole],
            out_specs=[pl.BlockSpec((ranks, block_rows, wide), lambda i, _: (0, i, 0)) for _, wide in shares[1:]]
            + [pl.BlockSpec((block_rows, wide), lambda i, _: (i, 0)) for _, wide in shares for _ in range(ranks)],
            scratch_shapes=[pltpu.VMEM((length, features), jnp.bfloat16)] * 2
            + [pltpu.SemaphoreType.DMA((2, steps))],
        ),
        out_shape=[result((ranks, length, wide), False) for _, wide in shares[1:]]
        + [result((length, wide), c == 0 and k) for c, (_, wide) in enumerate(shares) for k in range(ranks)],
        compiler_params=params(14),
        cost_estimate=cost(4 * inputs.size, 8 * inputs.size),
    )(rank, pinned(upstream), pinned(inputs))
    normed = outs[len(shares) - 1 :]
    return outs[: len(shares) - 1], [normed[c * ranks : (c + 1) * ranks] for c in range(len(shares))]


def folded(x):
    return jnp.sum(x.reshape(x.shape[0] // 8, 8, x.shape[1]), axis=0)


def attention_kernel(ranks, rank_ref, *refs):
    normed_refs, grad_out_refs = refs[:ranks], refs[ranks : 2 * ranks]
    keys_ref, values_ref, gain_ref = refs[2 * ranks : 2 * ranks + 3]
    *grad_queries_refs, grad_keys_ref, grad_values_ref, grad_gain_ref = refs[-ranks - 10 : -7]
    normed_ref, out_ref, turned_ref, weights_ref, slopes_ref, value_sums, key_sums = refs[-7:]
    tokens = grad_queries_refs[0].shape[0]
    length, wide = keys_ref.shape
    block = min(BLOCK, length)
    blocks = length // block
    scaling = 1.0 / math.sqrt(HEAD_DIM)
    base = scaling * math.log2(math.e)

    def rows_of(k):
        return pl.ds(pl.multiple_of((rank_ref[0] ^ k) * tokens, tokens), tokens)

    for k in range(ranks):
        normed_ref[rows_of(k), :] = normed_refs[k][...]
        out_ref[rows_of(k), :] = grad_out_refs[k][0] if k == 0 else grad_out_refs[k][...]

    key_at = lax.broadcasted_iota(jnp.int32, (block, block), 0)
    query_at = lax.broadcasted_iota(jnp.int32, (block, block), 1)
    allowed = key_at <= query_at
    across = (((1,), (1,)), ((), ()))

    def rows(x, i):
        return x[i * block : (i + 1) * block]

    heads = []
    for n, start in enumerate(range(0, wide, HEAD_DIM)):
        at = slice(start, start + HEAD_DIM)
        keys = keys_ref[:, at]
        heads.append(
            dict(
                n=n,
                at=at,
                queries=(normed_ref[:, at].astype(jnp.float32) * gain_ref[:, at]).astype(jnp.bfloat16),
                grad_out=out_ref[:, at],
                keys=keys,
                values=values_ref[:, at],
                keys_turned=keys.T,
            )
        )

    def product(head, i, j):
        score = lax.dot_general(
            rows(head["keys"], j), rows(head["queries"], i), across, preferred_element_type=jnp.float32
        )
        weighed = lax.dot_general(
            rows(head["values"], j), rows(head["grad_out"], i), across, preferred_element_type=jnp.float32
        )
        score = jnp.where(allowed, score, -jnp.inf) if j == i else score
        return score, weighed, jnp.max(score.reshape(block // 8, 8, block), axis=0)

    def joined(x, y):
        return y if x is None else x + y

    def gradients(head, i):
        here, upto = slice(i * block, (i + 1) * block), slice(0, (i + 1) * block)
        held, at = head["n"], head["at"]
        weights, slopes = weights_ref[held, upto, here], slopes_ref[held, upto, here]
        turned = jnp.dot(head["keys_turned"][:, upto], slopes, preferred_element_type=jnp.float32)
        turned_ref[here, at] = turned.T.astype(jnp.bfloat16)
        for sums_ref, grad_ref, wide, x in (
            (value_sums, grad_values_ref, weights, head["grad_out"]),
            (key_sums, grad_keys_ref, slopes, head["queries"]),
        ):
            part = jnp.dot(wide, rows(x, i), preferred_element_type=jnp.float32)
            if i < blocks - 1:
                part = part + sums_ref[upto, at]
            grad_ref[here, at] = part[here].astype(jnp.bfloat16)
            if i:
                before = slice(0, i * block)
                sums_ref[before, at] = part[before]

    stages = [(head, i) for head in heads for i in reversed(range(blocks))]
    ready = [product(*stages[0], j) for j in range(stages[0][1] + 1)]
    for at, (head, i) in enumerate(stages):
        tiles, ready = ready, []
        later = [(*stages[at + 1], j) for j in range(stages[at + 1][1] + 1)] if at + 1 < len(stages) else []
        top = functools.reduce(jnp.maximum, [t[2] for t in tiles])
        shift = jnp.max(top, axis=0, keepdims=True) * base
        exps, total, slope = [], None, None
        for j, (score, weighed, _) in enumerate(tiles):
            e = jnp.exp2(score * base - shift)
            exps.append(e)
            total = joined(total, folded(e))
            slope = joined(slope, folded(e * weighed))
            if later:
                ready.append(product(*later.pop(0)))
        ready += [product(*one) for one in later]
        if at:
            gradients(*stages[at - 1])
        inverse = 1.0 / jnp.sum(total, axis=0, keepdims=True)
        delta = jnp.sum(slope, axis=0, keepdims=True) * inverse
        for j, (_, weighed, _) in enumerate(tiles):
            weights = exps[j] * inverse
            spot = (head["n"], slice(j * block, (j + 1) * block), slice(i * block, (i + 1) * block))
            weights_ref[spot] = weights.astype(jnp.bfloat16)
            slopes_ref[spot] = (weights * (weighed - delta) * scaling).astype(jnp.bfloat16)
    gradients(*stages[-1])

    grad_gain_ref[...] = jnp.sum(
        folded(turned_ref[...].astype(jnp.float32) * normed_ref[...].astype(jnp.float32)), axis=0, keepdims=True
    )
    for k, grad_queries_ref in enumerate(grad_queries_refs):
        grad_queries_ref[...] = turned_ref[rows_of(k), :]


def attention_back(share, rank, normed, grad_out, keys, values, gain, earlier):
    start, wide = share
    heads = wide // HEAD_DIM
    step = math.gcd(math.gcd(start, wide), HEADS_A_STEP * HEAD_DIM)
    first = start // step
    ranks, tokens = len(normed), normed[0].shape[0]
    length = keys.shape[0]
    own = pl.BlockSpec((tokens, step), lambda h, _: (0, h))
    first_piece = pl.BlockSpec((1, tokens, step), lambda h, _: (0, 0, h))
    placed = pl.BlockSpec((length, step), lambda h, _: (0, first + h))
    pairs = length * length * heads
    outs = pl.pallas_call(
        functools.partial(attention_kernel, ranks),
        grid_spec=pltpu.PrefetchScalarGridSpec(
            num_scalar_prefetch=1,
            grid=(wide // step,),
            in_specs=[own] * ranks
            + [first_piece]
            + [own] * (ranks - 1)
            + [placed, placed, pl.BlockSpec((1, step), lambda h, _: (0, first + h))]
            + [pl.BlockSpec(memory_space=pl.ANY)] * len(earlier),
            out_specs=[own] * ranks
            + [placed, placed, pl.BlockSpec((1, step), lambda h, _: (0, h))],
            scratch_shapes=[pltpu.VMEM((length, step), jnp.bfloat16)] * 3
            + [pltpu.VMEM((step // HEAD_DIM, length, length), jnp.bfloat16)] * 2
            + [pltpu.VMEM((length, step), jnp.float32)] * 2,
        ),
        out_shape=[made((tokens, wide))] * ranks
        + [pltpu.HBM(keys.shape, jnp.bfloat16)] * 2
        + [made((1, wide), jnp.float32)],
        input_output_aliases={2 * ranks + 4 + i: ranks + i for i in range(len(earlier))},
        compiler_params=params(20),
        cost_estimate=cost(10 * pairs * HEAD_DIM, 8 * pairs, pairs),
    )(rank, *normed, *grad_out, pinned(keys), pinned(values), gain, *earlier)
    return outs[:ranks], outs[ranks : ranks + 2], outs[-1]


def lanes(x):
    return sum(x[:, i : i + HEAD_DIM] for i in range(0, x.shape[1], HEAD_DIM))


def wide_piece(share, ranks, rank_ref, k, inputs_ref, gain_ref, grad_ref):
    start, wide = share
    columns = inputs_ref.shape[1] // ranks
    at = pl.ds(pl.multiple_of((rank_ref[0] ^ k) * columns + start, HEAD_DIM), wide)
    x = inputs_ref[:, at].astype(jnp.float32)
    return at, x, grad_ref[...].astype(jnp.float32) * gain_ref[:, at]


def begin_kernel(shares, ranks, rank_ref, inputs_ref, gain_ref, *refs):
    given, (inverse_ref, products_ref), base_refs = refs[: -len(shares) - 2], refs[-len(shares) - 2 : -len(shares)], refs[-len(shares) :]
    incoming_refs, grad_refs = given[: len(shares)], given[len(shares) :][::-1]
    x = inputs_ref[...].astype(jnp.float32)
    squares = lanes(x * x)
    mean = jnp.sum(squares, axis=-1, keepdims=True) / inputs_ref.shape[1]
    inverse = 1.0 / jnp.sqrt(mean + EPSILON)
    products = jnp.zeros(products_ref.shape, jnp.float32)
    for c, share in enumerate(shares):
        for k in range(ranks):
            _, x, scaled = wide_piece(share, ranks, rank_ref, k, inputs_ref, gain_ref, grad_refs[c * ranks + k])
            products += lanes(scaled * (x * inverse))
            base_refs[c][k] = incoming_refs[c][k].astype(jnp.float32) + scaled * inverse
    inverse_ref[...] = jnp.broadcast_to(inverse, inverse_ref.shape)
    products_ref[...] = products


def finish_kernel(shares, ranks, rank_ref, inputs_ref, gain_ref, inverse_ref, products_ref, *refs):
    *base_refs, incoming_ref = refs[: len(shares)]
    grad_refs, out_ref = refs[len(shares) : -1][::-1], refs[-1]
    features = inputs_ref.shape[1]
    inverse = inverse_ref[:, :1]
    products, last = products_ref[...], []
    for k in range(ranks):
        last.append(wide_piece(shares[-1], ranks, rank_ref, k, inputs_ref, gain_ref, grad_refs[k]))
        products += lanes(last[k][2] * (last[k][1] * inverse))
    slope = jnp.sum(products, axis=-1, keepdims=True) / features * inverse * inverse
    for (start, wide), base_ref in zip(shares, base_refs):
        for k in range(ranks):
            at = pl.ds(pl.multiple_of((rank_ref[0] ^ k) * (features // ranks) + start, HEAD_DIM), wide)
            out_ref[:, at] = (base_ref[k] - inputs_ref[:, at].astype(jnp.float32) * slope).astype(jnp.bfloat16)
    for k, (at, x, scaled) in enumerate(last):
        incoming = incoming_ref[k].astype(jnp.float32)
        out_ref[:, at] = (incoming + (scaled * inverse - x * slope)).astype(jnp.bfloat16)


def finish(rank, inputs, gain, incoming, grads, shares, block_rows):
    length, features = inputs.shape
    ranks = len(grads[0])
    flat = pl.BlockSpec((block_rows, features), lambda i, _: (i, 0))
    row = pl.BlockSpec((1, features), lambda i, _: (0, 0))
    narrow = pl.BlockSpec((block_rows, HEAD_DIM), lambda i, _: (i, 0))
    stacks = [pl.BlockSpec((ranks, block_rows, wide), lambda i, _: (0, i, 0)) for _, wide in shares]
    pieces = [[pl.BlockSpec((block_rows, wide), lambda i, _: (i, 0))] * ranks for _, wide in shares]
    before = len(shares) - 1

    def call(kernel, in_specs, out_specs, out_shape, share):
        return pl.pallas_call(
            functools.partial(kernel, shares[:before] if kernel is begin_kernel else shares, ranks),
            grid_spec=pltpu.PrefetchScalarGridSpec(
                num_scalar_prefetch=1, grid=(length // block_rows,), in_specs=in_specs, out_specs=out_specs
            ),
            out_shape=out_shape,
            compiler_params=params(20),
            cost_estimate=cost(12 * inputs.size, share * inputs.size),
        )

    inverse, products, *base = call(
        begin_kernel,
        [flat, row] + stacks[:before] + sum(pieces[:before], [])[::-1],
        [narrow, narrow] + stacks[:before],
        [made((length, HEAD_DIM), jnp.float32)] * 2
        + [made((ranks, length, wide), jnp.float32) for _, wide in shares[:before]],
        10,
    )(rank, inputs, gain, *incoming[:before], *sum(grads[:before], [])[::-1])
    result = call(
        finish_kernel,
        [flat, row, narrow, narrow] + stacks + pieces[before],
        flat,
        made(inputs.shape),
        6,
    )(rank, inputs, gain, inverse, products, *base, incoming[before], *grads[before][::-1])
    return result, inverse


def from_behind(x, axis, by):
    devices = lax.axis_size(axis)
    return lax.ppermute(x, axis, [(i, (i + by) % devices) for i in range(devices)])


def total(x, axis, events):
    passing, result = x, x
    for _ in range(lax.axis_size(axis) - 1):
        passing = from_behind(passing, axis, 1)
        result = result + after([passing], events)[0]
    return result


def after(values, events):
    return lax.optimization_barrier((tuple(values), tuple(events)))[0]


def swap(x, k):
    return lax.ppermute(x, "tensor", [(i, i ^ k) for i in range(lax.axis_size("tensor"))])


def swapped(pieces, earlier=None):
    results = [pieces[0]]
    for k, piece in enumerate(pieces[1:], 1):
        if earlier and piece is not None:
            (piece,) = after([piece], earlier[k : k + 1])
        results.append(piece if piece is None else swap(piece, k))
    return results


def body(upstream, inputs, keys, values, gain):
    ranks = lax.axis_size("tensor")
    tokens = inputs.shape[2]
    columns = keys.shape[3]
    shares = cut(columns)

    upstream, inputs = upstream[0, 0], inputs[0, 0]
    keys, values = keys[0, 0], values[0, 0]
    rank = lax.axis_index("tensor")
    gain_columns = lax.dynamic_slice_in_dim(gain, rank * columns, columns, 1)
    rank = rank[None]

    first = lead(rank, upstream, shares[0], ranks)
    (later,) = after([rank], [first])
    handed, normed = prepare(later, upstream, inputs, shares, ranks, min(64, tokens))
    latest = None
    for c, pieces in enumerate(normed):
        normed[c] = latest = swapped(pieces, latest)
    incoming = []
    for c, held in enumerate([first, *handed]):
        if c >= 2:
            (held,) = after([held], [incoming[c - 2]])
        incoming.append(from_behind(held, "pipe", -1))
    grad_out = []
    for held in incoming:
        latest = swapped([held] + [held[k] for k in range(1, ranks)], latest)
        grad_out.append(latest)

    grads, gain_parts, earlier = [], [], ()
    for c, share in enumerate(shares):
        if 0 < c < len(shares) - 1:
            grad_out[c] = list(after(grad_out[c], [incoming[c + 1]]))
        grad_queries, earlier, gain_part = attention_back(
            share, rank, normed[c], grad_out[c], keys, values, gain_columns, earlier
        )
        gain_parts.append(gain_part)
        ahead = grads[-1] if grads else None
        grads.append(swapped(grad_queries, ahead))
    grad_keys, grad_values = earlier
    (inputs,) = after([inputs], gain_parts[-1:])
    grad_inputs, begun = finish(rank, inputs, gain, incoming, grads, shares, min(128, tokens))
    grad_gain = total(jnp.concatenate(gain_parts, axis=1), "dp", [begun])
    return (
        grad_inputs[None, None],
        grad_keys[None, None],
        grad_values[None, None],
        grad_gain,
    )


def solution(mesh):
    in_specs = (
        P("pipe", "dp", "tensor", None),
        P("pipe", "dp", "tensor", None),
        P("pipe", "dp", None, "tensor"),
        P("pipe", "dp", None, "tensor"),
        P("pipe", None),
    )
    out_specs = (
        P("pipe", "dp", "tensor", None),
        P("pipe", "dp", None, "tensor"),
        P("pipe", "dp", None, "tensor"),
        P("pipe", "tensor"),
    )
    return jax.shard_map(body, mesh=mesh, in_specs=in_specs, out_specs=out_specs, check_vma=False)
```

time: 130 us -> 122 us (0.938)
  starting transfers between devices: 31.5 us -> 23.9 us
  Pallas kernels: 47.2 us -> 49.9 us
  local copies, waits for them, and re-layouts: 4.42 us -> 2.32 us
    ppermute x27, starting transfers between devices: 23.9 us -> 16.4 us  [swap(): lax.ppermute(x, 'tensor', [(i, i ^ k) for i in range(lax.axis_size('tenso...]
    ppermute x4, waiting for transfers between devices: 12.9 us -> 7.83 us  [from_behind(): lax.ppermute(x, axis, [(i, (i + by) % devices) for i in range(devices)])]
    ppermute x27, waiting for transfers between devices: 31.8 us -> 36.4 us  [swap(): lax.ppermute(x, 'tensor', [(i, i ^ k) for i in range(lax.axis_size('tenso...]
    pallas_call x1 -> x3, Pallas kernels: 4.74 us -> 7.88 us  [the longest x1 3.44 us: finish(): call(begin_kernel, [flat, row] + stacks[:before] + sum(pieces[:before], [...]
    unnamed x36 -> x24, local copies, waits for them, and re-layouts: 4.26 us -> 2.11 us
  transfers between devices with their start and end apart: 31 -> 31, of which waited for: 12 -> 12; matrix products, arithmetic and copies ran while one was open for 1% -> 1% of each run, Pallas kernels for 29% -> 37%
where the time goes in v2:
time: 122 us
  Pallas kernels  49.9 us (41%)
  waiting for transfers between devices  44.2 us (36%)
  starting transfers between devices  23.9 us (20%)
  local copies, waits for them, and re-layouts  2.32 us (2%)
    pallas_call x3, Pallas kernels, attention_back(): pl.pallas_call(functools.partial(attention_kernel, ranks), grid_spec=pltp...  37.1 us
    ppermute x27, waiting for transfers between devices, swap(): lax.ppermute(x, 'tensor', [(i, i ^ k) for i in range(lax.axis_size('tenso...  36.4 us
    ppermute x27, starting transfers between devices, swap(): lax.ppermute(x, 'tensor', [(i, i ^ k) for i in range(lax.axis_size('tenso...  16.4 us
    ppermute x4, waiting for transfers between devices, from_behind(): lax.ppermute(x, axis, [(i, (i + by) % devices) for i in range(devices)])  7.83 us
    ppermute x4, starting transfers between devices, from_behind(): lax.ppermute(x, axis, [(i, (i + by) % devices) for i in range(devices)])  7.54 us
    pallas_call x1, Pallas kernels, prepare(): pl.pallas_call(functools.partial(prepare_kernel, shares, ranks, steps), g...  4.98 us
    pallas_call x1, Pallas kernels, finish(): call(begin_kernel, [flat, row] + stacks[:before] + sum(pieces[:before], [...  3.44 us
    pallas_call x1, Pallas kernels, finish(): call(finish_kernel, [flat, row, narrow, narrow] + stacks + pieces[before]...  3.2 us
  transfers between devices with their start and end apart: 31, of which 12 were waited for; matrix products, arithmetic and copies ran while one was open for 1% of the time, Pallas kernels for 37%

profile of v2, /device:TPU:0, one launch (start us, length us, event | category | flops | bytes accessed | tf_op | source)
XLA Modules:
  0.0 121.8 jit_solution(5123637964185559308)
XLA Ops:
  0.6 1.2 %shard_map.84 = bf16[4,256,512]{2,1,0:T(8,128)(2,1)S(1)} custom-call(s32[1]{0:T(128)} %bitcast.rank_ref, bf16[256,6144]{1,0:T(8,128)(2,1)} %bitcast.29), custom_call_target="tpu_custom_call" | custom-call | bytes 1572864 | tf_op jit(solution)/shard_map/pallas_call | solution.py:56
  1.9 5.1 %collective-permute-start.9 = (bf16[4,256,512]{2,1,0:T(8,128)(2,1)S(1)}, bf16[4,256,512]{2,1,0:T(8,128)(2,1)S(1)}, u32[]{:S(2)}, u32[]{:S(2)}) collective-permute-start(bf16[4,256,512]{2,1,0:T(8,128)(2,1)S(1)} %shard_map.84), channel_id=1, source_target_pairs={{0,12},{4,0},{8,4},{12,8},{1,13},{5,1},{9,5},{13,9},{2,14},{6,2},{... | collective-permute-start | bytes 3145736 | tf_op jit(solution)/shard_map/ppermute | solution.py:374
  7.0 5.0 %shard_map.85 = (bf16[4,256,640]{2,1,0:T(8,128)(2,1)}, bf16[4,256,384]{2,1,0:T(8,128)(2,1)}, bf16[256,512]{1,0:T(8,128)(2,1)}, bf16[256,512]{1,0:T(8,128)(2,1)S(...) custom-call(s32[1]{0:T(128)} %bitcast.rank_ref, ...), custom_call_target="tpu_custom_call" | custom-call | flops 6291456 | bytes 12582912 | tf_op jit(solution)/shard_map/pallas_call | solution.py:116
  12.9 1.2 collective-permute-start.3
  14.3 6.7 %collective-permute-done.6.refs_3_ = bf16[256,512]{1,0:T(8,128)(2,1)S(1)} collective-permute-done((bf16[256,512]{1,0:T(8,128)(2,1)S(1)}, bf16[256,512]{1,0:T(8,128)(2,1)S(1)}, u32[]{:S(2)}, u32[]{:S(2)}) %collective-permute-start.6) | collective-permute-done | bytes 262176 | tf_op jit(solution)/shard_map/ppermute | solution.py:390
  21.0 0.7 copy-done.4
  22.0 4.8 %collective-permute-done.3.refs_2_ = bf16[256,512]{1,0:T(8,128)(2,1)S(1)} collective-permute-done((bf16[256,512]{1,0:T(8,128)(2,1)S(1)}, bf16[256,512]{1,0:T(8,128)(2,1)S(1)}, u32[]{:S(2)}, u32[]{:S(2)}) %collective-permute-start.3) | collective-permute-done | bytes 262176 | tf_op jit(solution)/shard_map/ppermute | solution.py:390
  26.8 0.7 copy-done.6
  27.9 0.7 copy-done.8
  28.6 0.8 collective-permute-start.1
  29.4 4.4 %collective-permute-done.7.refs_3_ = bf16[256,640]{1,0:T(8,128)(2,1)} collective-permute-done((bf16[256,640]{1,0:T(8,128)(2,1)}, bf16[256,640]{1,0:T(8,128)(2,1)}, u32[]{:S(2)}, u32[]{:S(2)}) %collective-permute-start.7) | collective-permute-done | bytes 327712 | tf_op jit(solution)/shard_map/ppermute | solution.py:390
  34.0 6.9 %collective-permute-done.4.refs_2_ = bf16[256,640]{1,0:T(8,128)(2,1)} collective-permute-done((bf16[256,640]{1,0:T(8,128)(2,1)}, bf16[256,640]{1,0:T(8,128)(2,1)}, u32[]{:S(2)}, u32[]{:S(2)}) %collective-permute-start.4) | collective-permute-done | bytes 327712 | tf_op jit(solution)/shard_map/ppermute | solution.py:390
  41.3 0.7 collective-permute-start.2
  42.1 2.8 %collective-permute-done.8.refs_3_ = bf16[256,384]{1,0:T(8,128)(2,1)S(1)} collective-permute-done((bf16[256,384]{1,0:T(8,128)(2,1)}, bf16[256,384]{1,0:T(8,128)(2,1)S(1)}, u32[]{:S(2)}, u32[]{:S(2)}) %collective-permute-start.8) | collective-permute-done | bytes 196640 | tf_op jit(solution)/shard_map/ppermute | solution.py:390
  45.2 4.1 %collective-permute-done.5.refs_2_ = bf16[256,384]{1,0:T(8,128)(2,1)S(1)} collective-permute-done((bf16[256,384]{1,0:T(8,128)(2,1)}, bf16[256,384]{1,0:T(8,128)(2,1)S(1)}, u32[]{:S(2)}, u32[]{:S(2)}) %collective-permute-start.5) | collective-permute-done | bytes 196640 | tf_op jit(solution)/shard_map/ppermute | solution.py:390
  49.7 0.8 collective-permute-start.12
  50.9 7.8 %collective-permute-done.11.refs_4_.refs_1_ = bf16[4,256,640]{2,1,0:T(8,128)(2,1)S(1)} collective-permute-done((bf16[4,256,640]{2,1,0:T(8,128)(2,1)}, bf16[4,256,640]{2,1,0:T(8,128)(2,1)S(1)}, u32[]{:S(2)}, u32[]{:S(2)}) %collective-permute-start.11) | collective-permute-done | bytes 1310752 | tf_op jit(solution)/shard_map/ppermute | solution.py:374
  58.9 1.5 %collective-permute-done.15.refs_6_ = bf16[256,512]{1,0:T(8,128)(2,1)S(1)} collective-permute-done((bf16[256,512]{1,0:T(8,128)(2,1)S(1)}, bf16[256,512]{1,0:T(8,128)(2,1)S(1)}, u32[]{:S(2)}, u32[]{:S(2)}) %collective-permute-start.15) | collective-permute-done | bytes 262176 | tf_op jit(solution)/shard_map/ppermute | solution.py:390
  61.2 12.4 %shard_map.86 = (bf16[256,512]{1,0:T(8,128)(2,1)S(1)}, bf16[256,512]{1,0:T(8,128)(2,1)S(1)}, bf16[256,512]{1,0:T(8,128)(2,1)S(1)}, bf16[256,512]{1,0:T(8,128)(2,...) custom-call(s32[1]{0:T(128)} %bitcast.rank_ref, ...), custom_call_target="tpu_custom_call" | custom-call | flops 5368709120 | bytes 33554432 | tf_op jit(solution)/shard_map/pallas_call | solution.py:259
  73.9 1.5 %collective-permute-start.23 = (bf16[256,512]{1,0:T(8,128)(2,1)S(1)}, bf16[256,512]{1,0:T(8,128)(2,1)S(1)}, u32[]{:S(2)}, u32[]{:S(2)}) collective-permute-start(bf16[256,512]{1,0:T(8,128)(2,1)S(1)} %get-tuple-element.117), channel_id=1, source_target_pairs={{0,2},{1,3},{2,0},{3,1},{4,6},{5,7},{6,4},{7,5},{8,10},{9,11},{10,... | collective-permute-start | bytes 786440 | tf_op jit(solution)/shard_map/ppermute | solution.py:390
  76.0 1.8 %collective-permute-start.20 = (bf16[256,384]{1,0:T(8,128)(2,1)S(1)}, bf16[256,384]{1,0:T(8,128)(2,1)S(1)}, u32[]{:S(2)}, u32[]{:S(2)}) collective-permute-start(bf16[256,384]{1,0:T(8,128)(2,1)S(1)} %get-tuple-element.100), channel_id=1, source_target_pairs={{0,3},{1,2},{2,1},{3,0},{4,7},{5,6},{6,5},{7,4},{8,11},{9,10},{10,... | collective-permute-start | bytes 589832 | tf_op jit(solution)/shard_map/ppermute | solution.py:390
  78.0 14.8 %shard_map.87 = (bf16[256,640]{1,0:T(8,128)(2,1)S(1)}, bf16[256,640]{1,0:T(8,128)(2,1)S(1)}, bf16[256,640]{1,0:T(8,128)(2,1)S(1)}, bf16[256,640]{1,0:T(8,128)(2,...) custom-call(s32[1]{0:T(128)} %bitcast.rank_ref, ...), custom_call_target="tpu_custom_call", output_to_operand_aliasing={{4}: (12, {}), {5}: (13, {})} | custom-call | flops 6710886400 | bytes 41943040 | tf_op jit(solution)/shard_map/pallas_call | solution.py:259
  93.3 2.0 %collective-permute-start.24 = (bf16[256,640]{1,0:T(8,128)(2,1)S(1)}, bf16[256,640]{1,0:T(8,128)(2,1)S(1)}, u32[]{:S(2)}, u32[]{:S(2)}) collective-permute-start(bf16[256,640]{1,0:T(8,128)(2,1)S(1)} %get-tuple-element.118), channel_id=1, source_target_pairs={{0,2},{1,3},{2,0},{3,1},{4,6},{5,7},{6,4},{7,5},{8,10},{9,11},{10,... | collective-permute-start | bytes 983048 | tf_op jit(solution)/shard_map/ppermute | solution.py:390
  95.3 1.4 %collective-permute-done.17.refs_6_ = bf16[256,384]{1,0:T(8,128)(2,1)S(1)} collective-permute-done((bf16[256,384]{1,0:T(8,128)(2,1)S(1)}, bf16[256,384]{1,0:T(8,128)(2,1)S(1)}, u32[]{:S(2)}, u32[]{:S(2)}) %collective-permute-start.17) | collective-permute-done | bytes 196640 | tf_op jit(solution)/shard_map/ppermute | solution.py:390
  96.7 9.8 %shard_map.88 = (bf16[256,384]{1,0:T(8,128)(2,1)S(1)}, bf16[256,384]{1,0:T(8,128)(2,1)S(1)}, bf16[256,384]{1,0:T(8,128)(2,1)S(1)}, bf16[256,384]{1,0:T(8,128)(2,...) custom-call(s32[1]{0:T(128)} %bitcast.rank_ref, ...), custom_call_target="tpu_custom_call", output_to_operand_aliasing={{4}: (12, {}), {5}: (13, {})} | custom-call | flops 4026531840 | bytes 25165824 | tf_op jit(solution)/shard_map/pallas_call | solution.py:259
  106.5 1.2 collective-permute-start.28
  107.7 2.7 %collective-permute-done.22.refs_2_ = bf16[256,640]{1,0:T(8,128)(2,1)S(1)} collective-permute-done((bf16[256,640]{1,0:T(8,128)(2,1)S(1)}, bf16[256,640]{1,0:T(8,128)(2,1)S(1)}, u32[]{:S(2)}, u32[]{:S(2)}) %collective-permute-start.22) | collective-permute-done | bytes 327712 | tf_op jit(solution)/shard_map/ppermute | solution.py:390
  110.4 1.9 %collective-permute-start.27 = (bf16[256,384]{1,0:T(8,128)(2,1)S(1)}, bf16[256,384]{1,0:T(8,128)(2,1)S(1)}, u32[]{:S(2)}, u32[]{:S(2)}) collective-permute-start(bf16[256,384]{1,0:T(8,128)(2,1)S(1)} %get-tuple-element.129), channel_id=1, source_target_pairs={{0,3},{1,2},{2,1},{3,0},{4,7},{5,6},{6,5},{7,4},{8,11},{9,10},{10,... | collective-permute-start | bytes 589832 | tf_op jit(solution)/shard_map/ppermute | solution.py:390
  112.3 1.5 %collective-permute-start.30 = (f32[1,1536]{1,0:T(1,128)S(1)}, f32[1,1536]{1,0:T(1,128)S(1)}, u32[]{:S(2)}, u32[]{:S(2)}) collective-permute-start(f32[1,1536]{1,0:T(1,128)S(1)} %constant_dynamic-update-slice_fusion), channel_id=1, source_target_pairs={{0,16},{16,0},{1,17},{17,1},{2,18},{18,2},{3,19},{19,3},{4,20},{20... | collective-permute-start | bytes 18440 | tf_op jit(solution)/shard_map/ppermute | solution.py:374
  113.8 3.4 %shard_map.89 = (f32[256,128]{1,0:T(8,128)S(1)}, f32[256,128]{1,0:T(8,128)S(1)}, f32[4,256,512]{2,1,0:T(8,128)S(1)}, f32[4,256,640]{2,1,0:T(8,128)S(1)}) custom-call(s32[1]{0:T(128)} %bitcast.rank_ref, bf16[256,6144]{1,0:T(8,128)(2,1)S(1)} %bitcast.27, f32[1,6144]{1,0:T(1,128)S(1)} %copy-done.1, ...), custom_call_target="tpu_custom_call" | custom-call | flops 18874368 | bytes 15728640 | tf_op jit(solution)/shard_map/pallas_call | solution.py:354
  117.9 0.7 collective-permute-done.27.refs_3_
  118.6 3.2 %shard_map.90 = bf16[256,6144]{1,0:T(8,128)(2,1)} custom-call(s32[1]{0:T(128)} %bitcast.rank_ref, bf16[256,6144]{1,0:T(8,128)(2,1)S(1)} %bitcast.28, f32[1,6144]{1,0:T(1,128)S(1)} %copy-done.1, f32[256,128]{1,0:T(8,128)S(1)} %get-tuple-element.124.inverse_ref, f32[256,128]{1,0:T(8,128)S(1)} %get-tuple-element.125.products_ref, ...), custom_call_target="tpu_custom_call" | custom-call | flops 18874368 | bytes 9437184 | tf_op jit(solution)/shard_map/pallas_call | solution.py:362
  (67 shorter events, 6.9 us)
Async XLA Ops:
  1.9 40.2 %collective-permute-start.9 = (bf16[4,256,512]{2,1,0:T(8,128)(2,1)S(1)}, bf16[4,256,512]{2,1,0:T(8,128)(2,1)S(1)}, u32[]{:S(2)}, u32[]{:S(2)}) collective-permute-start(bf16[4,256,512]{2,1,0:T(8,128)(2,1)S(1)} %shard_map.84), channel_id=1, source_target_pairs={{0,12},{4,0},{8,4},{12,8},{1,13},{5,1},{9,5},{13,9},{2,14},{6,2},{... | collective-permute-start | bytes 3145736 | tf_op jit(solution)/shard_map/ppermute | solution.py:374
  7.0 43.5 %copy-start.1 = (f32[1,6144]{1,0:T(1,128)S(1)}, f32[1,6144]{1,0:T(1,128)}, u32[]{:S(2)}) copy-start(f32[1,6144]{1,0:T(1,128)} %gain_ref.3) | copy-start | bytes 73732
  12.0 46.8 %collective-permute-start.11 = (bf16[4,256,640]{2,1,0:T(8,128)(2,1)}, bf16[4,256,640]{2,1,0:T(8,128)(2,1)S(1)}, u32[]{:S(2)}, u32[]{:S(2)}) collective-permute-start(bf16[4,256,640]{2,1,0:T(8,128)(2,1)} %get-tuple-element.91), channel_id=1, source_target_pairs={{0,12},{4,0},{8,4},{12,8},{1,13},{5,1},{9,5},{13,9},{2,14},{6,2},{... | collective-permute-start | bytes 3932168 | tf_op jit(solution)/shard_map/ppermute | solution.py:374
  12.5 8.5 %collective-permute-start.6 = (bf16[256,512]{1,0:T(8,128)(2,1)S(1)}, bf16[256,512]{1,0:T(8,128)(2,1)S(1)}, u32[]{:S(2)}, u32[]{:S(2)}) collective-permute-start(bf16[256,512]{1,0:T(8,128)(2,1)S(1)} %get-tuple-element.86), channel_id=1, source_target_pairs={{0,3},{1,2},{2,1},{3,0},{4,7},{5,6},{6,5},{7,4},{8,11},{9,10},{10,... | collective-permute-start | bytes 786440 | tf_op jit(solution)/shard_map/ppermute | solution.py:390
  12.9 13.9 %collective-permute-start.3 = (bf16[256,512]{1,0:T(8,128)(2,1)S(1)}, bf16[256,512]{1,0:T(8,128)(2,1)S(1)}, u32[]{:S(2)}, u32[]{:S(2)}) collective-permute-start(bf16[256,512]{1,0:T(8,128)(2,1)S(1)} %get-tuple-element.81), channel_id=1, source_target_pairs={{0,2},{1,3},{2,0},{3,1},{4,6},{5,7},{6,4},{7,5},{8,10},{9,11},{10,... | collective-permute-start | bytes 786440 | tf_op jit(solution)/shard_map/ppermute | solution.py:390
  14.0 13.9 %collective-permute-start = (bf16[256,512]{1,0:T(8,128)(2,1)S(1)}, bf16[256,512]{1,0:T(8,128)(2,1)S(1)}, u32[]{:S(2)}, u32[]{:S(2)}) collective-permute-start(bf16[256,512]{1,0:T(8,128)(2,1)S(1)} %get-tuple-element.76), channel_id=1, source_target_pairs={{0,1},{1,0},{2,3},{3,2},{4,5},{5,4},{6,7},{7,6},{8,9},{9,8},{10,11... | collective-permute-start | bytes 786440 | tf_op jit(solution)/shard_map/ppermute | solution.py:390
  21.7 12.1 %collective-permute-start.7 = (bf16[256,640]{1,0:T(8,128)(2,1)}, bf16[256,640]{1,0:T(8,128)(2,1)}, u32[]{:S(2)}, u32[]{:S(2)}) collective-permute-start(bf16[256,640]{1,0:T(8,128)(2,1)} %get-tuple-element.87), channel_id=1, source_target_pairs={{0,3},{1,2},{2,1},{3,0},{4,7},{5,6},{6,5},{7,4},{8,11},{9,10},{10,... | collective-permute-start | bytes 983048 | tf_op jit(solution)/shard_map/ppermute | solution.py:390
  27.4 13.5 %collective-permute-start.4 = (bf16[256,640]{1,0:T(8,128)(2,1)}, bf16[256,640]{1,0:T(8,128)(2,1)}, u32[]{:S(2)}, u32[]{:S(2)}) collective-permute-start(bf16[256,640]{1,0:T(8,128)(2,1)} %get-tuple-element.82), channel_id=1, source_target_pairs={{0,2},{1,3},{2,0},{3,1},{4,6},{5,7},{6,4},{7,5},{8,10},{9,11},{10,... | collective-permute-start | bytes 983048 | tf_op jit(solution)/shard_map/ppermute | solution.py:390
  28.6 12.8 %collective-permute-start.1 = (bf16[256,640]{1,0:T(8,128)(2,1)}, bf16[256,640]{1,0:T(8,128)(2,1)}, u32[]{:S(2)}, u32[]{:S(2)}) collective-permute-start(bf16[256,640]{1,0:T(8,128)(2,1)} %get-tuple-element.77), channel_id=1, source_target_pairs={{0,1},{1,0},{2,3},{3,2},{4,5},{5,4},{6,7},{7,6},{8,9},{9,8},{10,11... | collective-permute-start | bytes 983048 | tf_op jit(solution)/shard_map/ppermute | solution.py:390
  33.7 11.1 %collective-permute-start.8 = (bf16[256,384]{1,0:T(8,128)(2,1)}, bf16[256,384]{1,0:T(8,128)(2,1)S(1)}, u32[]{:S(2)}, u32[]{:S(2)}) collective-permute-start(bf16[256,384]{1,0:T(8,128)(2,1)} %get-tuple-element.88), channel_id=1, source_target_pairs={{0,3},{1,2},{2,1},{3,0},{4,7},{5,6},{6,5},{7,4},{8,11},{9,10},{10,... | collective-permute-start | bytes 589832 | tf_op jit(solution)/shard_map/ppermute | solution.py:390
  40.9 8.3 %collective-permute-start.5 = (bf16[256,384]{1,0:T(8,128)(2,1)}, bf16[256,384]{1,0:T(8,128)(2,1)S(1)}, u32[]{:S(2)}, u32[]{:S(2)}) collective-permute-start(bf16[256,384]{1,0:T(8,128)(2,1)} %get-tuple-element.83), channel_id=1, source_target_pairs={{0,2},{1,3},{2,0},{3,1},{4,6},{5,7},{6,4},{7,5},{8,10},{9,11},{10,... | collective-permute-start | bytes 589832 | tf_op jit(solution)/shard_map/ppermute | solution.py:390
  41.3 8.3 %collective-permute-start.2 = (bf16[256,384]{1,0:T(8,128)(2,1)}, bf16[256,384]{1,0:T(8,128)(2,1)S(1)}, u32[]{:S(2)}, u32[]{:S(2)}) collective-permute-start(bf16[256,384]{1,0:T(8,128)(2,1)} %get-tuple-element.78), channel_id=1, source_target_pairs={{0,1},{1,0},{2,3},{3,2},{4,5},{5,4},{6,7},{7,6},{8,9},{9,8},{10,11... | collective-permute-start | bytes 589832 | tf_op jit(solution)/shard_map/ppermute | solution.py:390
  44.9 13.9 %collective-permute-start.18 = (bf16[256,512]{1,0:T(8,128)(2,1)S(1)}, bf16[256,512]{1,0:T(8,128)(2,1)S(1)}, u32[]{:S(2)}, u32[]{:S(2)}) collective-permute-start(bf16[256,512]{1,0:T(8,128)(2,1)S(1)} %get-tuple-element.98), channel_id=1, source_target_pairs={{0,3},{1,2},{2,1},{3,0},{4,7},{5,6},{6,5},{7,4},{8,11},{9,10},{10,... | collective-permute-start | bytes 786440 | tf_op jit(solution)/shard_map/ppermute | solution.py:390
  49.2 11.2 %collective-permute-start.15 = (bf16[256,512]{1,0:T(8,128)(2,1)S(1)}, bf16[256,512]{1,0:T(8,128)(2,1)S(1)}, u32[]{:S(2)}, u32[]{:S(2)}) collective-permute-start(bf16[256,512]{1,0:T(8,128)(2,1)S(1)} %get-tuple-element.95), channel_id=1, source_target_pairs={{0,2},{1,3},{2,0},{3,1},{4,6},{5,7},{6,4},{7,5},{8,10},{9,11},{10,... | collective-permute-start | bytes 786440 | tf_op jit(solution)/shard_map/ppermute | solution.py:390
  49.7 11.2 %collective-permute-start.12 = (bf16[256,512]{1,0:T(8,128)(2,1)S(1)}, bf16[256,512]{1,0:T(8,128)(2,1)S(1)}, u32[]{:S(2)}, u32[]{:S(2)}) collective-permute-start(bf16[256,512]{1,0:T(8,128)(2,1)S(1)} %get-tuple-element.92), channel_id=1, source_target_pairs={{0,1},{1,0},{2,3},{3,2},{4,5},{5,4},{6,7},{7,6},{8,9},{9,8},{10,11... | collective-permute-start | bytes 786440 | tf_op jit(solution)/shard_map/ppermute | solution.py:390
  50.5 25.5 %collective-permute-start.10 = (bf16[4,256,384]{2,1,0:T(8,128)(2,1)}, bf16[4,256,384]{2,1,0:T(8,128)(2,1)S(1)}, u32[]{:S(2)}, u32[]{:S(2)}) collective-permute-start(bf16[4,256,384]{2,1,0:T(8,128)(2,1)} %get-tuple-element.90), channel_id=1, source_target_pairs={{0,12},{4,0},{8,4},{12,8},{1,13},{5,1},{9,5},{13,9},{2,14},{6,2},{... | collective-permute-start | bytes 2359304 | tf_op jit(solution)/shard_map/ppermute | solution.py:374
  58.8 15.0 %collective-permute-start.19 = (bf16[256,640]{1,0:T(8,128)(2,1)S(1)}, bf16[256,640]{1,0:T(8,128)(2,1)S(1)}, u32[]{:S(2)}, u32[]{:S(2)}) collective-permute-start(bf16[256,640]{1,0:T(8,128)(2,1)S(1)} %get-tuple-element.99), channel_id=1, source_target_pairs={{0,3},{1,2},{2,1},{3,0},{4,7},{5,6},{6,5},{7,4},{8,11},{9,10},{10,... | collective-permute-start | bytes 983048 | tf_op jit(solution)/shard_map/ppermute | solution.py:390
  60.4 15.5 %collective-permute-start.16 = (bf16[256,640]{1,0:T(8,128)(2,1)S(1)}, bf16[256,640]{1,0:T(8,128)(2,1)S(1)}, u32[]{:S(2)}, u32[]{:S(2)}) collective-permute-start(bf16[256,640]{1,0:T(8,128)(2,1)S(1)} %get-tuple-element.96), channel_id=1, source_target_pairs={{0,2},{1,3},{2,0},{3,1},{4,6},{5,7},{6,4},{7,5},{8,10},{9,11},{10,... | collective-permute-start | bytes 983048 | tf_op jit(solution)/shard_map/ppermute | solution.py:390
  60.9 15.1 %collective-permute-start.13 = (bf16[256,640]{1,0:T(8,128)(2,1)S(1)}, bf16[256,640]{1,0:T(8,128)(2,1)S(1)}, u32[]{:S(2)}, u32[]{:S(2)}) collective-permute-start(bf16[256,640]{1,0:T(8,128)(2,1)S(1)} %get-tuple-element.93), channel_id=1, source_target_pairs={{0,1},{1,0},{2,3},{3,2},{4,5},{5,4},{6,7},{7,6},{8,9},{9,8},{10,11... | collective-permute-start | bytes 983048 | tf_op jit(solution)/shard_map/ppermute | solution.py:390
  73.7 4.2 %collective-permute-start.25 = (bf16[256,512]{1,0:T(8,128)(2,1)S(1)}, bf16[256,512]{1,0:T(8,128)(2,1)S(1)}, u32[]{:S(2)}, u32[]{:S(2)}) collective-permute-start(bf16[256,512]{1,0:T(8,128)(2,1)S(1)} %get-tuple-element.120), channel_id=1, source_target_pairs={{0,1},{1,0},{2,3},{3,2},{4,5},{5,4},{6,7},{7,6},{8,9},{9,8},{10,11... | collective-permute-start | bytes 786440 | tf_op jit(solution)/shard_map/ppermute | solution.py:390
  73.9 19.0 %collective-permute-start.23 = (bf16[256,512]{1,0:T(8,128)(2,1)S(1)}, bf16[256,512]{1,0:T(8,128)(2,1)S(1)}, u32[]{:S(2)}, u32[]{:S(2)}) collective-permute-start(bf16[256,512]{1,0:T(8,128)(2,1)S(1)} %get-tuple-element.117), channel_id=1, source_target_pairs={{0,2},{1,3},{2,0},{3,1},{4,6},{5,7},{6,4},{7,5},{8,10},{9,11},{10,... | collective-permute-start | bytes 786440 | tf_op jit(solution)/shard_map/ppermute | solution.py:390
  75.9 17.3 %collective-permute-start.21 = (bf16[256,512]{1,0:T(8,128)(2,1)S(1)}, bf16[256,512]{1,0:T(8,128)(2,1)S(1)}, u32[]{:S(2)}, u32[]{:S(2)}) collective-permute-start(bf16[256,512]{1,0:T(8,128)(2,1)S(1)} %get-tuple-element.114), channel_id=1, source_target_pairs={{0,3},{1,2},{2,1},{3,0},{4,7},{5,6},{6,5},{7,4},{8,11},{9,10},{10,... | collective-permute-start | bytes 786440 | tf_op jit(solution)/shard_map/ppermute | solution.py:390
  76.0 19.2 %collective-permute-start.20 = (bf16[256,384]{1,0:T(8,128)(2,1)S(1)}, bf16[256,384]{1,0:T(8,128)(2,1)S(1)}, u32[]{:S(2)}, u32[]{:S(2)}) collective-permute-start(bf16[256,384]{1,0:T(8,128)(2,1)S(1)} %get-tuple-element.100), channel_id=1, source_target_pairs={{0,3},{1,2},{2,1},{3,0},{4,7},{5,6},{6,5},{7,4},{8,11},{9,10},{10,... | collective-permute-start | bytes 589832 | tf_op jit(solution)/shard_map/ppermute | solution.py:390
  77.8 18.8 %collective-permute-start.17 = (bf16[256,384]{1,0:T(8,128)(2,1)S(1)}, bf16[256,384]{1,0:T(8,128)(2,1)S(1)}, u32[]{:S(2)}, u32[]{:S(2)}) collective-permute-start(bf16[256,384]{1,0:T(8,128)(2,1)S(1)} %get-tuple-element.97), channel_id=1, source_target_pairs={{0,2},{1,3},{2,0},{3,1},{4,6},{5,7},{6,4},{7,5},{8,10},{9,11},{10,... | collective-permute-start | bytes 589832 | tf_op jit(solution)/shard_map/ppermute | solution.py:390
  77.9 18.8 %collective-permute-start.14 = (bf16[256,384]{1,0:T(8,128)(2,1)S(1)}, bf16[256,384]{1,0:T(8,128)(2,1)S(1)}, u32[]{:S(2)}, u32[]{:S(2)}) collective-permute-start(bf16[256,384]{1,0:T(8,128)(2,1)S(1)} %get-tuple-element.94), channel_id=1, source_target_pairs={{0,1},{1,0},{2,3},{3,2},{4,5},{5,4},{6,7},{7,6},{8,9},{9,8},{10,11... | collective-permute-start | bytes 589832 | tf_op jit(solution)/shard_map/ppermute | solution.py:390
  92.9 13.6 %collective-permute-start.26 = (bf16[256,640]{1,0:T(8,128)(2,1)S(1)}, bf16[256,640]{1,0:T(8,128)(2,1)S(1)}, u32[]{:S(2)}, u32[]{:S(2)}) collective-permute-start(bf16[256,640]{1,0:T(8,128)(2,1)S(1)} %get-tuple-element.121), channel_id=1, source_target_pairs={{0,1},{1,0},{2,3},{3,2},{4,5},{5,4},{6,7},{7,6},{8,9},{9,8},{10,11... | collective-permute-start | bytes 983048 | tf_op jit(solution)/shard_map/ppermute | solution.py:390
  93.3 13.2 %collective-permute-start.24 = (bf16[256,640]{1,0:T(8,128)(2,1)S(1)}, bf16[256,640]{1,0:T(8,128)(2,1)S(1)}, u32[]{:S(2)}, u32[]{:S(2)}) collective-permute-start(bf16[256,640]{1,0:T(8,128)(2,1)S(1)} %get-tuple-element.118), channel_id=1, source_target_pairs={{0,2},{1,3},{2,0},{3,1},{4,6},{5,7},{6,4},{7,5},{8,10},{9,11},{10,... | collective-permute-start | bytes 983048 | tf_op jit(solution)/shard_map/ppermute | solution.py:390
  95.3 15.1 %collective-permute-start.22 = (bf16[256,640]{1,0:T(8,128)(2,1)S(1)}, bf16[256,640]{1,0:T(8,128)(2,1)S(1)}, u32[]{:S(2)}, u32[]{:S(2)}) collective-permute-start(bf16[256,640]{1,0:T(8,128)(2,1)S(1)} %get-tuple-element.115), channel_id=1, source_target_pairs={{0,3},{1,2},{2,1},{3,0},{4,7},{5,6},{6,5},{7,4},{8,11},{9,10},{10,... | collective-permute-start | bytes 983048 | tf_op jit(solution)/shard_map/ppermute | solution.py:390
  106.5 11.4 %collective-permute-start.29 = (bf16[256,384]{1,0:T(8,128)(2,1)S(1)}, bf16[256,384]{1,0:T(8,128)(2,1)S(1)}, u32[]{:S(2)}, u32[]{:S(2)}) collective-permute-start(bf16[256,384]{1,0:T(8,128)(2,1)S(1)} %get-tuple-element.133), channel_id=1, source_target_pairs={{0,1},{1,0},{2,3},{3,2},{4,5},{5,4},{6,7},{7,6},{8,9},{9,8},{10,11... | collective-permute-start | bytes 589832 | tf_op jit(solution)/shard_map/ppermute | solution.py:390
  106.5 11.4 %collective-permute-start.28 = (bf16[256,384]{1,0:T(8,128)(2,1)S(1)}, bf16[256,384]{1,0:T(8,128)(2,1)S(1)}, u32[]{:S(2)}, u32[]{:S(2)}) collective-permute-start(bf16[256,384]{1,0:T(8,128)(2,1)S(1)} %get-tuple-element.131), channel_id=1, source_target_pairs={{0,2},{1,3},{2,0},{3,1},{4,6},{5,7},{6,4},{7,5},{8,10},{9,11},{10,... | collective-permute-start | bytes 589832 | tf_op jit(solution)/shard_map/ppermute | solution.py:390
  110.4 8.2 %collective-permute-start.27 = (bf16[256,384]{1,0:T(8,128)(2,1)S(1)}, bf16[256,384]{1,0:T(8,128)(2,1)S(1)}, u32[]{:S(2)}, u32[]{:S(2)}) collective-permute-start(bf16[256,384]{1,0:T(8,128)(2,1)S(1)} %get-tuple-element.129), channel_id=1, source_target_pairs={{0,3},{1,2},{2,1},{3,0},{4,7},{5,6},{6,5},{7,4},{8,11},{9,10},{10,... | collective-permute-start | bytes 589832 | tf_op jit(solution)/shard_map/ppermute | solution.py:390
  112.3 4.9 %collective-permute-start.30 = (f32[1,1536]{1,0:T(1,128)S(1)}, f32[1,1536]{1,0:T(1,128)S(1)}, u32[]{:S(2)}, u32[]{:S(2)}) collective-permute-start(f32[1,1536]{1,0:T(1,128)S(1)} %constant_dynamic-update-slice_fusion), channel_id=1, source_target_pairs={{0,16},{16,0},{1,17},{17,1},{2,18},{18,2},{3,19},{19,3},{4,20},{20... | collective-permute-start | bytes 18440 | tf_op jit(solution)/shard_map/ppermute | solution.py:374
  (10 other events, 182.0 us)
